TPU v7x, 32 devices: a whole 2x2x4 slice. The times are simulated.
32 devices in a mesh: node: 8 (over y, x, core), local: 4 (over z).
Axes of the slice: x: 2, y: 2, z: 4, core: 2. Of those that a mesh axis runs over, the one named last changes fastest.
Arguments:
- activations: bfloat16 [4096, 4096], P(('node', 'local')), may hold values from -6 to 6
- codes: bfloat16 [16, 256, 128], P('local'), may hold values from -127 to 127, as said below
- scales: float32 [16, 128], P('local'), may hold values from 5e-05 to 0.0005
- cotangent: bfloat16 [4096, 128], P(('node', 'local')), may hold values from -6 to 6
Outputs:
- values_out: bfloat16 [4096, 128], P(('node', 'local'))
- weight_grad: float32 [4096, 128], P(('node', 'local'))
Inputs may be any that keep to these rules, and one draw needn't show every extreme that they name: codes are whole numbers.
All inputs are finite; a program needn't handle non-finite values.
Results may differ from a plain program's by a relative error of at most 0.0048.
Values may be sent and summed in bfloat16 or wider, within the bound.
A program may use at most 64 MiB of HBM per device.

v0:
```python
import jax
import jax.numpy as jnp
from jax import lax
from jax.sharding import PartitionSpec as P


def on_device(activations, codes, scales, cotangent):
    head_width = codes.shape[2]
    stored = (
        (codes.astype(jnp.float32) * scales[:, None, :])
        .astype(jnp.bfloat16)
        .reshape(-1, head_width)
    )
    projected = jnp.dot(
        activations,
        lax.all_gather(stored, "local", axis=0, tiled=True),
        preferred_element_type=jnp.float32,
    )
    values_out = projected.astype(jnp.bfloat16)
    node_count = lax.axis_size("node")
    local_count = lax.axis_size("local")
    token_total = activations.shape[0] * node_count * local_count
    term = lax.dot_general(
        activations, cotangent, (((0,), (0,)), ((), ())), preferred_element_type=jnp.float32
    )
    term = term * float(token_total) ** (-0.5)
    width = term.shape[0]
    share = width // (node_count * local_count)
    shaped = term.reshape(node_count, local_count, share, head_width)
    partial_value = lax.psum_scatter(shaped, "local", scatter_dimension=1, tiled=True)
    finished = lax.psum_scatter(partial_value, "node", scatter_dimension=0, tiled=True)
    weight_grad = finished.reshape(share, head_width)
    return (values_out, weight_grad)


def solution(mesh):
    in_specs = (
        P(("node", "local"), None),
        P("local", None, None),
        P("local", None),
        P(("node", "local"), None),
    )
    out_specs = (P(("node", "local"), None), P(("node", "local"), None))
    return jax.shard_map(
        on_device, mesh=mesh, in_specs=in_specs, out_specs=out_specs, check_vma=False
    )
```

profile of v0, /device:TPU:0, one launch (start us, length us, event | category | flops | bytes accessed | tf_op | source)
XLA Modules:
  0.0 173.1 jit_solution(8244199105294225166)
XLA Ops:
  7.2 0.0 copy-start
  7.2 0.0 copy-start.1
  7.2 0.0 copy-start.2
  7.2 0.0 all-reduce.3.cloned.1.call-start
  7.2 1.1 copy-done
  8.4 2.5 %convolution_multiply_fusion = f32[4096,128]{1,0:T(8,128)} fusion(bf16[128,4096]{1,0:T(8,128)(2,1)S(1)} %copy-done, bf16[128,128]{1,0:T(8,128)(2,1)} %param.7), kind=kOutput, calls=%fused_computation | convolution fusion | flops 134742016 | bytes 3178496 | tf_op jit(solution)/shard_map/dot_general | solution.py:23
  10.9 0.0 copy-start.3
  10.9 0.0 all-reduce.3.cloned.1.call-update
  11.0 0.0 all-gather.2.cloned.1.call-start
  11.0 0.0 copy-done.1
  11.0 0.0 copy-done.2
  11.0 0.8 multiply_convert_fusion
  11.8 0.0 all-gather.2.cloned.1.call-update
  11.8 0.0 reduce-scatter.5.cloned.1.call-start
  11.9 0.0 copy-done.3
  11.9 0.6 dynamic-slice
  12.5 87.9 %all-reduce.3.cloned.1.call-done = f32[8,4,128,128]{3,2,1,0:T(8,128)} async-done(((f32[8,4,128,128]{3,2,1,0:T(8,128)}), f32[8,4,128,128]{3,2,1,0:T(8,128)}) %all-reduce.3.cloned.1.call-update) | async-done | bytes 2097168
  100.3 2.5 %constant_dynamic-slice_fusion = f32[8,1,128,128]{3,2,1,0:T(8,128)} fusion(f32[8,4,128,128]{3,2,1,0:T(8,128)} %all-reduce.3.cloned.1.call-done, u32[]{:T(128)} %bitcast.10), kind=kLoop, calls=%fused_computation.4 | loop fusion | bytes 1048580
  102.9 0.0 reduce-scatter.5.cloned.1.call-update
  102.9 26.0 %all-gather.2.cloned.1.call-done = bf16[4096,128]{1,0:T(8,128)(2,1)} async-done(((bf16[1024,128]{1,0:T(8,128)(2,1)}), bf16[4096,128]{1,0:T(8,128)(2,1)}) %all-gather.2.cloned.1.call-update) | async-done | bytes 1048592 | tf_op jit(solution)/shard_map/all_gather | solution.py:16
  128.9 1.7 fusion
  130.6 0.7 copy.7
  131.3 35.2 %reduce-scatter.5.cloned.1.call-done = f32[1,1,128,128]{3,2,1,0:T(8,128)} async-done(((f32[8,1,128,128]{3,2,1,0:T(8,128)}), f32[1,1,128,128]{3,2,1,0:T(8,128)}) %reduce-scatter.5.cloned.1.call-update) | async-done | bytes 65552 | tf_op jit(solution)/shard_map/reduce_scatter | solution.py:31
Async XLA Ops:
  7.2 1.2 copy-start
  7.2 3.8 %copy-start.1 = (bf16[4,256,128]{2,1,0:T(8,128)(2,1)S(1)}, bf16[4,256,128]{2,1,0:T(8,128)(2,1)}, u32[]{:S(2)}) copy-start(bf16[4,256,128]{2,1,0:T(8,128)(2,1)} %param.5) | copy-start | bytes 786436
  7.2 3.8 %copy-start.2 = (f32[4,128]{1,0:T(4,128)S(1)}, f32[4,128]{1,0:T(4,128)}, u32[]{:S(2)}) copy-start(f32[4,128]{1,0:T(4,128)} %param.6) | copy-start | bytes 6148
  7.2 93.1 %all-reduce.3.cloned.1.call-start = ((), (), s32[]{:S(2)}) async-start(), calls=%async_computation.3 | async-start | bytes 4194304
  10.9 0.9 copy-start.3
  11.0 117.9 %all-gather.2.cloned.1.call-start = ((), (), s32[]{:S(2)}) async-start(), calls=%async_computation.1 | async-start | bytes 1310720 | tf_op jit(solution)/shard_map/all_gather | solution.py:16
  11.8 154.7 %reduce-scatter.5.cloned.1.call-start = ((), (), s32[]{:S(2)}) async-start(), calls=%async_computation.2 | async-start | bytes 589824 | tf_op jit(solution)/shard_map/reduce_scatter | solution.py:31
Sparse Core Ops, SparseCore 0:
  11.1 89.2 all-reduce.2
  102.0 26.8 all-gather.1
  132.9 33.6 reduce-scatter.4
where the time goes:
time: 173 us
  waiting for transfers between devices  149 us (86%)
  between operations  13.8 us (8%)
  local copies, waits for them, and re-layouts  5.01 us (3%)
  matrix products  4.24 us (2%)
    unnamed x4, waiting for transfers between devices  87.9 us
    reduce_scatter x1, waiting for transfers between devices, on_device(): lax.psum_scatter(partial_value, 'node', scatter_dimension=0, tiled=True)  35.2 us
    all_gather x1, waiting for transfers between devices, on_device(): lax.all_gather(stored, 'local', axis=0, tiled=True)  26 us
    unnamed x11, local copies, waits for them, and re-layouts  5.01 us
  transfers between devices with their start and end apart: 3, of which 3 were waited for; matrix products, arithmetic and copies ran while one was open for 4% of the time, Pallas kernels for 0%

commit v1 on v0

v1 whole, which is shorter than its diff:
```python
import functools

import jax
import jax.numpy as jnp
from jax import lax
from jax.experimental import pallas as pl
from jax.experimental.pallas import tpu as pltpu
from jax.sharding import PartitionSpec as P

MESH = pl.DeviceIdType.MESH
F32 = jnp.float32
BF16 = jnp.bfloat16


def aligned(value, unit):
    return pl.multiple_of(value * unit, unit)


def exchange_kernel(
    n_node, n_local, norm,
    act_hbm, codes_ref, scales_ref, cot_ref,
    values_ref, grad_ref,
    act, weight, act_in, cot_in, term_out, term_in,
    load_sem, act_send, act_recv, cot_send, cot_recv,
    w_send, w_recv, f_send, f_recv, g_send, g_recv,
):
    node, z = lax.axis_index("node"), lax.axis_index("local")
    pair, core = node // 2, node % 2
    n_pair = n_node // 2
    tok = act.shape[0]
    share = term_in.shape[1]
    blocks, block, width = codes_ref.shape
    rows = blocks * block
    half = rows // 2

    load = pltpu.make_async_copy(act_hbm, act, load_sem)
    load.start()

    peers = []
    for slot in range(1, n_node):
        to = ((pair + slot // 2) % n_pair) * 2 + (core + slot % 2) % 2
        peers.append((slot, to))
    line = [(k, (z + 1 + k) % n_local, (z + n_local - 1 - k) % n_local) for k in range(n_local - 1)]

    barrier = pltpu.get_barrier_semaphore()
    for _, to in peers:
        pl.semaphore_signal(barrier, inc=1, device_id=(to, z), device_id_type=MESH)
    for _, to, _ in line:
        pl.semaphore_signal(barrier, inc=1, device_id=(node, to), device_id_type=MESH)

    for b in range(blocks):
        part = codes_ref[b].astype(F32) * scales_ref[b : b + 1, :]
        weight[z, b * block : (b + 1) * block, :] = part.astype(BF16)
    cot_in[0:tok, :] = cot_ref[...]
    load.wait()
    pl.semaphore_wait(barrier, len(peers) + len(line))

    def cot_copy(slot, to):
        return pltpu.make_async_remote_copy(
            src_ref=cot_ref, dst_ref=cot_in.at[pl.ds(slot * tok, tok)],
            send_sem=cot_send.at[slot], recv_sem=cot_recv.at[slot],
            device_id=(to, z), device_id_type=MESH)

    def act_copy(k, slot, to):
        column = aligned(to * n_local + (z + 1 + k) % n_local, share)
        return pltpu.make_async_remote_copy(
            src_ref=act.at[:, pl.ds(column, share)],
            dst_ref=act_in.at[k, pl.ds(slot * tok, tok)],
            send_sem=act_send.at[k, slot], recv_sem=act_recv.at[k, slot],
            device_id=(to, z), device_id_type=MESH)

    def weight_copy(k, owner, to):
        ref = weight.at[owner, pl.ds(aligned(core, half), half)]
        return pltpu.make_async_remote_copy(
            src_ref=ref, dst_ref=ref, send_sem=w_send.at[k], recv_sem=w_recv.at[k],
            device_id=(node, to), device_id_type=MESH)

    def pass_copy(k, owner, which):
        ref = weight.at[owner, pl.ds(aligned(which, half), half)]
        return pltpu.make_async_remote_copy(
            src_ref=ref, dst_ref=ref, send_sem=f_send.at[k], recv_sem=f_recv.at[k],
            device_id=(pair * 2 + 1 - core, z), device_id_type=MESH)

    def term_copy(k, to):
        return pltpu.make_async_remote_copy(
            src_ref=term_out.at[k], dst_ref=term_in.at[k],
            send_sem=g_send.at[k], recv_sem=g_recv.at[k],
            device_id=(node, to), device_id_type=MESH)

    for slot, to in peers:
        cot_copy(slot, to).start()
    for k, to, _ in line:
        weight_copy(k, z, to).start()
    for k in range(n_local):
        for slot, to in peers:
            act_copy(k, slot, to).start()

    def projected(owner):
        return jnp.dot(act[:, pl.ds(aligned(owner, rows), rows)], weight[owner],
                       preferred_element_type=F32)

    total = projected(z)

    def group_term(k):
        column = aligned(node * n_local + (z + 1 + k) % n_local, share)
        act_in[k, 0:tok, :] = act[:, pl.ds(column, share)]
        for slot, to in peers:
            if k == 0:
                cot_copy(slot, to).wait_recv()
            act_copy(k, slot, to).wait_recv()
        return lax.dot_general(act_in[k], cot_in[...], (((0,), (0,)), ((), ())),
                               preferred_element_type=F32)

    for k, to, _ in line:
        term_out[k] = group_term(k)
        term_copy(k, to).start()
    for k, to, owner in line:
        weight_copy(k, owner, to).wait_recv()
        pass_copy(k, owner, core).start()
    grad = group_term(n_local - 1)
    for k, to, owner in line:
        pass_copy(k, owner, 1 - core).wait_recv()
        total += projected(owner)
    values_ref[...] = total.astype(BF16)
    for k, to, _ in line:
        term_copy(k, to).wait_recv()
        grad += term_in[k]
    grad_ref[...] = grad * norm

    for slot, to in peers:
        cot_copy(slot, to).wait_send()
        for k in range(n_local):
            act_copy(k, slot, to).wait_send()
    for k, to, owner in line:
        weight_copy(k, z, to).wait_send()
        pass_copy(k, owner, core).wait_send()
        term_copy(k, to).wait_send()


def exchanged(n_node, n_local, activations, codes, scales, cotangent):
    tok, width = activations.shape
    blocks, block, head = codes.shape
    rows = blocks * block
    share = width // (n_node * n_local)
    dma = pltpu.SemaphoreType.DMA
    vmem = pl.BlockSpec(memory_space=pltpu.VMEM)
    norm = float(tok * n_node * n_local) ** (-0.5)
    return pl.pallas_call(
        functools.partial(exchange_kernel, n_node, n_local, norm),
        out_shape=(
            jax.ShapeDtypeStruct((tok, head), BF16),
            jax.ShapeDtypeStruct((share, head), F32),
        ),
        in_specs=[pl.BlockSpec(memory_space=pl.ANY), vmem, vmem, vmem],
        out_specs=(vmem, vmem),
        scratch_shapes=[
            pltpu.VMEM((tok, width), BF16),
            pltpu.VMEM((n_local, rows, head), BF16),
            pltpu.VMEM((n_local, n_node * tok, share), BF16),
            pltpu.VMEM((n_node * tok, head), BF16),
            pltpu.VMEM((n_local, share, head), F32),
            pltpu.VMEM((n_local, share, head), F32),
            dma, dma((n_local, n_node)), dma((n_local, n_node)), dma((n_node,)), dma((n_node,)),
            dma((n_local,)), dma((n_local,)), dma((n_local,)), dma((n_local,)),
            dma((n_local,)), dma((n_local,)),
        ],
        compiler_params=pltpu.CompilerParams(
            collective_id=0, has_side_effects=True, vmem_limit_bytes=32 * 1024 * 1024
        ),
        cost_estimate=pl.CostEstimate(
            flops=4 * tok * width * head, bytes_accessed=2 * tok * width, transcendentals=0
        ),
    )(activations, codes, scales, cotangent)


def gathered(n_node, n_local, activations, codes, scales, cotangent):
    head = codes.shape[2]
    stored = (codes.astype(F32) * scales[:, None, :]).astype(BF16).reshape(-1, head)
    weight = lax.all_gather(stored, "local", axis=0, tiled=True)
    values = jnp.dot(activations, weight, preferred_element_type=F32).astype(BF16)
    term = lax.dot_general(
        activations, cotangent, (((0,), (0,)), ((), ())), preferred_element_type=F32
    )
    tokens = activations.shape[0] * n_node * n_local
    term = term * float(tokens) ** (-0.5)
    share = term.shape[0] // (n_node * n_local)
    term = term.reshape(n_node, n_local, share, head)
    term = lax.psum_scatter(term, "local", scatter_dimension=1, tiled=True)
    term = lax.psum_scatter(term, "node", scatter_dimension=0, tiled=True)
    return values, term.reshape(share, head)


def solution(mesh):
    n_node, n_local = mesh.shape["node"], mesh.shape["local"]

    def on_device(activations, codes, scales, cotangent):
        share = activations.shape[1] // (n_node * n_local)
        run = exchanged if share % 128 == 0 and n_node % 2 == 0 else gathered
        return run(n_node, n_local, activations, codes, scales, cotangent)

    return jax.shard_map(
        on_device,
        mesh=mesh,
        in_specs=(
            P(("node", "local"), None),
            P("local", None, None),
            P("local", None),
            P(("node", "local"), None),
        ),
        out_specs=(P(("node", "local"), None), P(("node", "local"), None)),
        check_vma=False,
    )
```

time: 173 us -> 31 us (0.18)
  waiting for transfers between devices: 149 us -> 0 us
  Pallas kernels: 0 us -> 25.2 us
  between operations: 13.8 us -> 0.65 us
  matrix products: 4.24 us -> 0 us
    unnamed x4 -> x0, waiting for transfers between devices: 87.9 us -> none
    reduce_scatter x1 -> x0, waiting for transfers between devices: 35.2 us -> none  [on_device(): lax.psum_scatter(partial_value, 'node', scatter_dimension=0, tiled=True)]
    all_gather x1 -> x0, waiting for transfers between devices: 26 us -> none  [on_device(): lax.all_gather(stored, 'local', axis=0, tiled=True)]
    pallas_call x0 -> x1, Pallas kernels: none -> 25.2 us  [exchanged(): pl.pallas_call(functools.partial(exchange_kernel, n_node, n_local, norm),...]
    dot_general x2 -> x0, matrix products: 4.24 us -> none  [the longest x1 2.54 us: on_device(): lax.dot_general(activations, cotangent, (((0,), (0,)), ((), ())), preferr...]
    unnamed x11 -> x10, local copies, waits for them, and re-layouts: 5.01 us -> 4.85 us
  transfers between devices with their start and end apart: 3 -> 0, of which waited for: 3 -> 0; matrix products, arithmetic and copies ran while one was open for 4% -> 0% of each run, Pallas kernels for 0% -> 0%
where the time goes in v1:
time: 31 us; the launch traced here: 30.7 us
  Pallas kernels  25.2 us (81%)
  local copies, waits for them, and re-layouts  4.85 us (16%)
  between operations  0.65 us (2%)
    pallas_call x1, Pallas kernels, exchanged(): pl.pallas_call(functools.partial(exchange_kernel, n_node, n_local, norm),...  25.2 us
    unnamed x10, local copies, waits for them, and re-layouts  4.85 us

profile of v1, /device:TPU:0, one launch (start us, length us, event | category | flops | bytes accessed | tf_op | source)
XLA Modules:
  0.0 30.7 jit_solution(7503168689744871611)
XLA Ops:
  0.6 0.0 copy-start
  0.6 1.2 %copy-done = bf16[128,4096]{1,0:T(8,128)(2,1)S(1)} copy-done((bf16[128,4096]{1,0:T(8,128)(2,1)S(1)}, bf16[128,4096]{1,0:T(8,128)(2,1)}, u32[]{:S(2)}) %copy-start) | copy-done | bytes 1048600
  1.9 0.0 copy-start.1
  1.9 0.9 %copy-done.1 = bf16[4,256,128]{2,1,0:T(8,128)(2,1)S(1)} copy-done((bf16[4,256,128]{2,1,0:T(8,128)(2,1)S(1)}, bf16[4,256,128]{2,1,0:T(8,128)(2,1)}, u32[]{:S(2)}) %copy-start.1) | copy-done | bytes 262168
  2.8 0.0 copy-start.2
  2.8 0.8 %copy-done.2 = bf16[128,128]{1,0:T(8,128)(2,1)S(1)} copy-done((bf16[128,128]{1,0:T(8,128)(2,1)S(1)}, bf16[128,128]{1,0:T(8,128)(2,1)}, u32[]{:S(2)}) %copy-start.2) | copy-done | bytes 32792
  3.6 0.0 copy-start.3
  3.6 0.7 %copy-done.3 = f32[4,128]{1,0:T(4,128)S(1)} copy-done((f32[4,128]{1,0:T(4,128)S(1)}, f32[4,128]{1,0:T(4,128)}, u32[]{:S(2)}) %copy-start.3) | copy-done | bytes 2072
  4.2 25.2 %shard_map.59 = (bf16[128,128]{1,0:T(8,128)(2,1)S(1)}, f32[128,128]{1,0:T(8,128)S(1)}) custom-call(bf16[128,4096]{1,0:T(8,128)(2,1)S(1)} %copy-done, bf16[4,256,128]{2,1,0:T(8,128)(2,1)S(1)} %copy-done.1, f32[4,128]{1,0:T(4,128)S(1)} %copy-done.3, bf16[128,128]{1,0:T(8,128)(2,1)S(1)} %copy-done.2), custom_call_target="tpu_custom_call" | custom-call | flops 268435456 | bytes 1048576 | tf_op jit(solution)/shard_map/pallas_call | solution.py:148
  29.5 0.6 %copy.8 = bf16[128,128]{1,0:T(8,128)(2,1)} copy(bf16[128,128]{1,0:T(8,128)(2,1)S(1)} %get-tuple-element.4) | data formatting | bytes 65536
  30.1 0.6 %copy.9 = f32[128,128]{1,0:T(8,128)} copy(f32[128,128]{1,0:T(8,128)S(1)} %get-tuple-element.5) | data formatting | bytes 131072
Async XLA Ops:
  0.6 1.2 %copy-start = (bf16[128,4096]{1,0:T(8,128)(2,1)S(1)}, bf16[128,4096]{1,0:T(8,128)(2,1)}, u32[]{:S(2)}) copy-start(bf16[128,4096]{1,0:T(8,128)(2,1)} %act_hbm.1) | copy-start | bytes 3145732
  1.9 0.9 %copy-start.1 = (bf16[4,256,128]{2,1,0:T(8,128)(2,1)S(1)}, bf16[4,256,128]{2,1,0:T(8,128)(2,1)}, u32[]{:S(2)}) copy-start(bf16[4,256,128]{2,1,0:T(8,128)(2,1)} %codes_ref.1) | copy-start | bytes 786436
  2.8 0.8 %copy-start.2 = (bf16[128,128]{1,0:T(8,128)(2,1)S(1)}, bf16[128,128]{1,0:T(8,128)(2,1)}, u32[]{:S(2)}) copy-start(bf16[128,128]{1,0:T(8,128)(2,1)} %cot_ref.1) | copy-start | bytes 98308
  3.6 0.7 %copy-start.3 = (f32[4,128]{1,0:T(4,128)S(1)}, f32[4,128]{1,0:T(4,128)}, u32[]{:S(2)}) copy-start(f32[4,128]{1,0:T(4,128)} %scales_ref.1) | copy-start | bytes 6148

commit v2 on v1

--- a/solution.py
+++ b/solution.py
@@ -18,9 +18,9 @@
 
 def exchange_kernel(
     n_node, n_local, norm,
-    act_hbm, codes_ref, scales_ref, cot_ref,
+    act_hbm, codes_hbm, scales_hbm, cot_hbm,
     values_ref, grad_ref,
-    act, weight, act_in, cot_in, term_out, term_in,
+    act, codes_ref, scales_ref, cot_ref, weight, act_in, cot_in, term_out, term_in,
     load_sem, act_send, act_recv, cot_send, cot_recv,
     w_send, w_recv, f_send, f_recv, g_send, g_recv,
 ):
@@ -33,8 +33,13 @@
     rows = blocks * block
     half = rows // 2
 
-    load = pltpu.make_async_copy(act_hbm, act, load_sem)
-    load.start()
+    loads = [
+        pltpu.make_async_copy(there, here, load_sem.at[i])
+        for i, (there, here) in enumerate((
+            (codes_hbm, codes_ref), (scales_hbm, scales_ref), (cot_hbm, cot_ref), (act_hbm, act)))
+    ]
+    for load in loads:
+        load.start()
 
     peers = []
     for slot in range(1, n_node):
@@ -48,11 +53,14 @@
     for _, to, _ in line:
         pl.semaphore_signal(barrier, inc=1, device_id=(node, to), device_id_type=MESH)
 
+    loads[0].wait()
+    loads[1].wait()
     for b in range(blocks):
         part = codes_ref[b].astype(F32) * scales_ref[b : b + 1, :]
         weight[z, b * block : (b + 1) * block, :] = part.astype(BF16)
+    loads[2].wait()
     cot_in[0:tok, :] = cot_ref[...]
-    load.wait()
+    loads[3].wait()
     pl.semaphore_wait(barrier, len(peers) + len(line))
 
     def cot_copy(slot, to):
@@ -151,16 +159,19 @@
             jax.ShapeDtypeStruct((tok, head), BF16),
             jax.ShapeDtypeStruct((share, head), F32),
         ),
-        in_specs=[pl.BlockSpec(memory_space=pl.ANY), vmem, vmem, vmem],
+        in_specs=[pl.BlockSpec(memory_space=pltpu.HBM)] * 4,
         out_specs=(vmem, vmem),
         scratch_shapes=[
             pltpu.VMEM((tok, width), BF16),
+            pltpu.VMEM(codes.shape, BF16),
+            pltpu.VMEM(scales.shape, F32),
+            pltpu.VMEM(cotangent.shape, BF16),
             pltpu.VMEM((n_local, rows, head), BF16),
             pltpu.VMEM((n_local, n_node * tok, share), BF16),
             pltpu.VMEM((n_node * tok, head), BF16),
             pltpu.VMEM((n_local, share, head), F32),
             pltpu.VMEM((n_local, share, head), F32),
-            dma, dma((n_local, n_node)), dma((n_local, n_node)), dma((n_node,)), dma((n_node,)),
+            dma((4,)), dma((n_local, n_node)), dma((n_local, n_node)), dma((n_node,)), dma((n_node,)),
             dma((n_local,)), dma((n_local,)), dma((n_local,)), dma((n_local,)),
             dma((n_local,)), dma((n_local,)),
         ],

time: 31 us -> 31.1 us (level)
  no operation moved by 1% of the time
where the time goes in v2:
time: 31.1 us; the launch traced here: 30.8 us
  Pallas kernels  25.3 us (81%)
  local copies, waits for them, and re-layouts  4.85 us (16%)
  between operations  0.65 us (2%)
    pallas_call x1, Pallas kernels, exchanged(): pl.pallas_call(functools.partial(exchange_kernel, n_node, n_local, norm),...  25.3 us
    unnamed x10, local copies, waits for them, and re-layouts  4.85 us

profile of v2, /device:TPU:0, one launch (start us, length us, event | category | flops | bytes accessed | tf_op | source)
XLA Modules:
  0.0 30.8 jit_solution(11289216907086894039)
XLA Ops:
  0.6 0.0 copy-start
  0.6 1.2 %copy-done = bf16[128,4096]{1,0:T(8,128)(2,1)S(1)} copy-done((bf16[128,4096]{1,0:T(8,128)(2,1)S(1)}, bf16[128,4096]{1,0:T(8,128)(2,1)}, u32[]{:S(2)}) %copy-start) | copy-done | bytes 1048600
  1.9 0.0 copy-start.1
  1.9 0.9 %copy-done.1 = bf16[4,256,128]{2,1,0:T(8,128)(2,1)S(1)} copy-done((bf16[4,256,128]{2,1,0:T(8,128)(2,1)S(1)}, bf16[4,256,128]{2,1,0:T(8,128)(2,1)}, u32[]{:S(2)}) %copy-start.1) | copy-done | bytes 262168
  2.8 0.0 copy-start.2
  2.8 0.8 %copy-done.2 = bf16[128,128]{1,0:T(8,128)(2,1)S(1)} copy-done((bf16[128,128]{1,0:T(8,128)(2,1)S(1)}, bf16[128,128]{1,0:T(8,128)(2,1)}, u32[]{:S(2)}) %copy-start.2) | copy-done | bytes 32792
  3.6 0.0 copy-start.3
  3.6 0.7 %copy-done.3 = f32[4,128]{1,0:T(4,128)S(1)} copy-done((f32[4,128]{1,0:T(4,128)S(1)}, f32[4,128]{1,0:T(4,128)}, u32[]{:S(2)}) %copy-start.3) | copy-done | bytes 2072
  4.2 25.3 %shard_map.59 = (bf16[128,128]{1,0:T(8,128)(2,1)S(1)}, f32[128,128]{1,0:T(8,128)S(1)}) custom-call(bf16[128,4096]{1,0:T(8,128)(2,1)S(1)} %copy-done, bf16[4,256,128]{2,1,0:T(8,128)(2,1)S(1)} %copy-done.1, f32[4,128]{1,0:T(4,128)S(1)} %copy-done.3, bf16[128,128]{1,0:T(8,128)(2,1)S(1)} %copy-done.2), custom_call_target="tpu_custom_call" | custom-call | flops 268435456 | bytes 1048576 | tf_op jit(solution)/shard_map/pallas_call | solution.py:156
  29.6 0.6 %copy.8 = bf16[128,128]{1,0:T(8,128)(2,1)} copy(bf16[128,128]{1,0:T(8,128)(2,1)S(1)} %get-tuple-element.4) | data formatting | bytes 65536
  30.2 0.6 %copy.9 = f32[128,128]{1,0:T(8,128)} copy(f32[128,128]{1,0:T(8,128)S(1)} %get-tuple-element.5) | data formatting | bytes 131072
Async XLA Ops:
  0.6 1.2 %copy-start = (bf16[128,4096]{1,0:T(8,128)(2,1)S(1)}, bf16[128,4096]{1,0:T(8,128)(2,1)}, u32[]{:S(2)}) copy-start(bf16[128,4096]{1,0:T(8,128)(2,1)} %act_hbm.1) | copy-start | bytes 3145732
  1.9 0.9 %copy-start.1 = (bf16[4,256,128]{2,1,0:T(8,128)(2,1)S(1)}, bf16[4,256,128]{2,1,0:T(8,128)(2,1)}, u32[]{:S(2)}) copy-start(bf16[4,256,128]{2,1,0:T(8,128)(2,1)} %codes_hbm.1) | copy-start | bytes 786436
  2.8 0.8 %copy-start.2 = (bf16[128,128]{1,0:T(8,128)(2,1)S(1)}, bf16[128,128]{1,0:T(8,128)(2,1)}, u32[]{:S(2)}) copy-start(bf16[128,128]{1,0:T(8,128)(2,1)} %cot_hbm.1) | copy-start | bytes 98308
  3.6 0.7 %copy-start.3 = (f32[4,128]{1,0:T(4,128)S(1)}, f32[4,128]{1,0:T(4,128)}, u32[]{:S(2)}) copy-start(f32[4,128]{1,0:T(4,128)} %scales_hbm.1) | copy-start | bytes 6148

commit v3 on v2

v3 whole, which is shorter than its diff:
```python
import functools

import jax
import jax.numpy as jnp
from jax import lax
from jax.experimental import pallas as pl
from jax.experimental.pallas import tpu as pltpu
from jax.sharding import PartitionSpec as P

MESH = pl.DeviceIdType.MESH
F32 = jnp.float32
BF16 = jnp.bfloat16


def aligned(value, unit):
    return pl.multiple_of(value * unit, unit)


def exchange_kernel(
    n_local, norm,
    act_hbm, codes_hbm, scales_hbm, cot_hbm,
    values_ref, grad_ref,
    act, codes_ref, scales_ref, cot_ref, weight, weight_in, act_in, cot_in,
    other_out, other_in, term_out, term_in,
    load_sem, act_send, act_recv, cot_send, cot_recv,
    w_send, w_recv, s_send, s_recv, g_send, g_recv,
):
    node, z = lax.axis_index("node"), lax.axis_index("local")
    y, x, core = node // 4, (node // 2) % 2, node % 2
    tok = act.shape[0]
    share = term_in.shape[1]
    blocks, block, _ = codes_ref.shape
    rows = blocks * block
    quarter = rows // 4
    eighth = quarter // 2
    last = n_local - 1

    loads = [
        pltpu.make_async_copy(there, here, load_sem.at[i])
        for i, (there, here) in enumerate((
            (codes_hbm, codes_ref), (scales_hbm, scales_ref), (cot_hbm, cot_ref), (act_hbm, act)))
    ]
    for load in loads:
        load.start()

    def at(to_y, to_x, to_core):
        return (to_y * 2 + to_x) * 2 + to_core

    partner = at(y, x, 1 - core)
    along_x = (at(y, 1 - x, core), at(y, 1 - x, 1 - core))
    along_y = (at(1 - y, x, core), at(1 - y, x, 1 - core))
    near = (partner,) + along_x + along_y
    line = [(k, (z + 1 + k) % n_local, (z + last - k) % n_local) for k in range(last)]

    barrier = pltpu.get_barrier_semaphore()
    for to in near:
        pl.semaphore_signal(barrier, inc=1, device_id=(to, z), device_id_type=MESH)
    for _, to, _ in line:
        pl.semaphore_signal(barrier, inc=1, device_id=(node, to), device_id_type=MESH)

    loads[0].wait()
    loads[1].wait()
    for b in range(blocks):
        part = codes_ref[b].astype(F32) * scales_ref[b : b + 1, :]
        weight[b * block : (b + 1) * block, :] = part.astype(BF16)
    loads[2].wait()
    cot_in[2 * tok : 3 * tok, :] = cot_ref[...]
    loads[3].wait()
    pl.semaphore_wait(barrier, len(near) + len(line))

    def send(src, dst, send_sem, recv_sem, to_node, to_local):
        return pltpu.make_async_remote_copy(
            src_ref=src, dst_ref=dst, send_sem=send_sem, recv_sem=recv_sem,
            device_id=(to_node, to_local), device_id_type=MESH)

    cot_copies = [
        send(cot_ref, cot_in.at[slot * tok : (slot + 1) * tok], cot_send.at[i], cot_recv.at[i], to, z)
        for i, (to, slot) in enumerate(zip(near, (3, 0, 1, 4, 5)))
    ]

    def column_of(k, owner):
        return pl.ds(aligned(owner * n_local + (z + 1 + k) % n_local, share), share)

    def second_of(k, owner_y, owner_x, owner_core):
        if k % 2 == 0:
            return at(1 - owner_y, owner_x, owner_core)
        return at(owner_y, 1 - owner_x, owner_core)

    def act_copies(k):
        over_x = k % 2 == 0
        first = (y, 1 - x) if over_x else (1 - y, x)
        own_row, first_row = (2, 0) if over_x else (0, 2)
        copies = []
        for i, (to_y, to_x, to_core, row) in enumerate((
            (first[0], first[1], core, first_row),
            (first[0], first[1], 1 - core, first_row + 1),
            (y, x, 1 - core, own_row + 1),
        )):
            to = at(to_y, to_x, to_core)
            for which, owner in ((1, second_of(k, to_y, to_x, to_core)), (0, to)):
                copies.append(send(
                    act.at[:, column_of(k, owner)],
                    act_in.at[k, which, row * tok : (row + 1) * tok],
                    act_send.at[k, 2 * i + which], act_recv.at[k, 2 * i + which], to, z))
        return copies

    def sum_copy(k):
        return send(other_out.at[k], other_in.at[k], s_send.at[k], s_recv.at[k],
                    second_of(k, y, x, core), z)

    def term_copy(k, to):
        return send(term_out.at[k], term_in.at[k], g_send.at[k], g_recv.at[k], node, to)

    parity = (x + y) % 2

    def part_of(of_parity, of_core, begin, size):
        return pl.ds(aligned((of_parity * 2 + of_core) * 2 + begin, eighth), size * eighth)

    def line_copy(k, to):
        part = part_of(parity, core, 0, 2)
        return send(weight.at[part], weight_in.at[k, part], w_send.at[0, k], w_recv.at[0, k], node, to)

    def plane_copies(k, of_parity):
        return [
            send(weight_in.at[k, part], weight_in.at[k, part],
                 w_send.at[1 + i, k], w_recv.at[1 + i, k], to, z)
            for i, (to, part) in enumerate((
                (along_x[0], part_of(of_parity, core, 0, 1)),
                (along_y[0], part_of(of_parity, core, 1, 1))))
        ]

    def pass_copy(k, i, of_parity, of_core):
        part = part_of(of_parity, of_core, 0, 2)
        return send(weight_in.at[k, part], weight_in.at[k, part],
                    w_send.at[3 + i, k], w_recv.at[3 + i, k], partner, z)

    for copy in cot_copies:
        copy.start()
    for k in range(min(2, n_local)):
        for copy in act_copies(k):
            copy.start()
    for k, to, _ in line:
        line_copy(k, to).start()

    def projected(owner, stored):
        return jnp.dot(act[:, pl.ds(aligned(owner, rows), rows)], stored, preferred_element_type=F32)

    total = projected(z, weight[...])

    def group_term(k):
        over_x = k % 2 == 0
        own_row = 2 if over_x else 0
        own = slice(own_row * tok, (own_row + 1) * tok)
        act_in[k, 1, own, :] = act[:, column_of(k, second_of(k, y, x, core))]
        act_in[k, 0, own, :] = act[:, column_of(k, node)]
        if k == 0:
            for copy in cot_copies:
                copy.wait_recv()
        for copy in act_copies(k):
            copy.wait_recv()
        if k + 2 < n_local:
            for copy in act_copies(k + 2):
                copy.start()
        cot = cot_in[0 : 4 * tok, :] if over_x else cot_in[2 * tok : 6 * tok, :]

        def product(which):
            return lax.dot_general(act_in[k, which], cot, (((0,), (0,)), ((), ())),
                                   preferred_element_type=F32)

        other_out[k] = product(1)
        sum_copy(k).start()
        term_out[k] = product(0)

    def finish_term(k):
        sum_copy(k).wait_recv()
        term_out[k] += other_in[k]
        if k < last:
            term_copy(k, line[k][1]).start()

    early = min(2, n_local)
    for k in range(early):
        group_term(k)
    for k, to, _ in line:
        line_copy(k, to).wait_recv()
        for copy in plane_copies(k, parity):
            copy.start()
        pass_copy(k, 0, parity, core).start()
    for k in range(early):
        finish_term(k)
    for k in range(early, n_local):
        group_term(k)
    for k, _, _ in line:
        for copy in plane_copies(k, 1 - parity):
            copy.wait_recv()
        pass_copy(k, 1, 1 - parity, core).start()
    for k in range(early, n_local):
        finish_term(k)
    for k, _, owner in line:
        pass_copy(k, 0, parity, 1 - core).wait_recv()
        pass_copy(k, 1, 1 - parity, 1 - core).wait_recv()
        total += projected(owner, weight_in[k])
    values_ref[...] = total.astype(BF16)
    grad = term_out[last]
    for k, to, _ in line:
        term_copy(k, to).wait_recv()
        grad += term_in[k]
    grad_ref[...] = grad * norm

    for copy in cot_copies:
        copy.wait_send()
    for k in range(n_local):
        for copy in act_copies(k):
            copy.wait_send()
        sum_copy(k).wait_send()
    for k, to, _ in line:
        line_copy(k, to).wait_send()
        for copy in plane_copies(k, parity):
            copy.wait_send()
        pass_copy(k, 0, parity, core).wait_send()
        pass_copy(k, 1, 1 - parity, core).wait_send()
        term_copy(k, to).wait_send()


def exchanged(n_node, n_local, activations, codes, scales, cotangent):
    tok, width = activations.shape
    blocks, block, head = codes.shape
    rows = blocks * block
    share = width // (n_node * n_local)
    dma = pltpu.SemaphoreType.DMA
    vmem = pl.BlockSpec(memory_space=pltpu.VMEM)
    norm = float(tok * n_node * n_local) ** (-0.5)
    piece = pltpu.VMEM((n_local, share, head), F32)
    return pl.pallas_call(
        functools.partial(exchange_kernel, n_local, norm),
        out_shape=(
            jax.ShapeDtypeStruct((tok, head), BF16),
            jax.ShapeDtypeStruct((share, head), F32),
        ),
        in_specs=[pl.BlockSpec(memory_space=pltpu.HBM)] * 4,
        out_specs=(vmem, vmem),
        scratch_shapes=[
            pltpu.VMEM((tok, width), BF16),
            pltpu.VMEM(codes.shape, BF16),
            pltpu.VMEM(scales.shape, F32),
            pltpu.VMEM(cotangent.shape, BF16),
            pltpu.VMEM((rows, head), BF16),
            pltpu.VMEM((n_local - 1, rows, head), BF16),
            pltpu.VMEM((n_local, 2, 4 * tok, share), BF16),
            pltpu.VMEM((6 * tok, head), BF16),
            piece, piece, piece, piece,
            dma((4,)), dma((n_local, 6)), dma((n_local, 6)), dma((5,)), dma((5,)),
            dma((5, n_local)), dma((5, n_local)), dma((n_local,)), dma((n_local,)),
            dma((n_local,)), dma((n_local,)),
        ],
        compiler_params=pltpu.CompilerParams(collective_id=0, has_side_effects=True),
        cost_estimate=pl.CostEstimate(
            flops=4 * tok * width * head, bytes_accessed=2 * tok * width, transcendentals=0
        ),
    )(activations, codes, scales, cotangent)


def gathered(n_node, n_local, activations, codes, scales, cotangent):
    head = codes.shape[2]
    stored = (codes.astype(F32) * scales[:, None, :]).astype(BF16).reshape(-1, head)
    weight = lax.all_gather(stored, "local", axis=0, tiled=True)
    values = jnp.dot(activations, weight, preferred_element_type=F32).astype(BF16)
    term = lax.dot_general(
        activations, cotangent, (((0,), (0,)), ((), ())), preferred_element_type=F32
    )
    tokens = activations.shape[0] * n_node * n_local
    term = term * float(tokens) ** (-0.5)
    share = term.shape[0] // (n_node * n_local)
    term = term.reshape(n_node, n_local, share, head)
    term = lax.psum_scatter(term, "local", scatter_dimension=1, tiled=True)
    term = lax.psum_scatter(term, "node", scatter_dimension=0, tiled=True)
    return values, term.reshape(share, head)


def solution(mesh):
    n_node, n_local = mesh.shape["node"], mesh.shape["local"]

    def on_device(activations, codes, scales, cotangent):
        share = activations.shape[1] // (n_node * n_local)
        rows = codes.shape[0] * codes.shape[1]
        fits = n_node == 8 and n_local > 1 and share % 128 == 0 and rows % 128 == 0
        run = exchanged if fits else gathered
        return run(n_node, n_local, activations, codes, scales, cotangent)

    return jax.shard_map(
        on_device,
        mesh=mesh,
        in_specs=(
            P(("node", "local"), None),
            P("local", None, None),
            P("local", None),
            P(("node", "local"), None),
        ),
        out_specs=(P(("node", "local"), None), P(("node", "local"), None)),
        check_vma=False,
    )
```

time: 31.1 us -> 28.9 us (0.929)
  local copies, waits for them, and re-layouts: 4.85 us -> 2.04 us
  Pallas kernels: 25.3 us -> 26 us
    unnamed x10 -> x4, local copies, waits for them, and re-layouts: 4.85 us -> 2.04 us
    pallas_call x1, Pallas kernels: 25.3 us -> 26 us  [exchanged(): pl.pallas_call(functools.partial(exchange_kernel, n_local, norm), out_sha...]
where the time goes in v3:
time: 28.9 us; the launch traced here: 28.7 us
  Pallas kernels  26 us (90%)
  local copies, waits for them, and re-layouts  2.04 us (7%)
  between operations  0.65 us (2%)
    pallas_call x1, Pallas kernels, exchanged(): pl.pallas_call(functools.partial(exchange_kernel, n_local, norm), out_sha...  26 us
    unnamed x4, local copies, waits for them, and re-layouts  2.04 us

profile of v3, /device:TPU:0, one launch (start us, length us, event | category | flops | bytes accessed | tf_op | source)
XLA Modules:
  0.0 28.7 jit_solution(12502415655281109696)
XLA Ops:
  0.6 26.0 %shard_map.59 = (bf16[128,128]{1,0:T(8,128)(2,1)}, f32[128,128]{1,0:T(8,128)}) custom-call(bf16[128,4096]{1,0:T(8,128)(2,1)} %act_hbm.1, bf16[4,256,128]{2,1,0:T(8,128)(2,1)} %codes_hbm.1, f32[4,128]{1,0:T(4,128)} %scales_hbm.1, bf16[128,128]{1,0:T(8,128)(2,1)} %cot_hbm.1), custom_call_target="tpu_custom_call" | custom-call | flops 268435456 | bytes 1048576 | tf_op jit(solution)/shard_map/pallas_call | solution.py:233
  26.6 0.0 copy-start
  26.6 1.4 %copy.8 = bf16[128,128]{1,0:T(8,128)(2,1)} copy(bf16[128,128]{1,0:T(8,128)(2,1)} %get-tuple-element.4) | data formatting | bytes 65536
  28.0 0.0 copy-done
  28.0 0.6 %copy.9 = f32[128,128]{1,0:T(8,128)} copy(f32[128,128]{1,0:T(8,128)S(1)} %copy-done) | data formatting | bytes 131072
Async XLA Ops:
  26.6 1.4 %copy-start = (f32[128,128]{1,0:T(8,128)S(1)}, f32[128,128]{1,0:T(8,128)}, u32[]{:S(2)}) copy-start(f32[128,128]{1,0:T(8,128)} %get-tuple-element.5) | copy-start | bytes 196612

commit v4 on v3

--- a/solution.py
+++ b/solution.py
@@ -20,7 +20,7 @@
     n_local, norm,
     act_hbm, codes_hbm, scales_hbm, cot_hbm,
     values_ref, grad_ref,
-    act, codes_ref, scales_ref, cot_ref, weight, weight_in, act_in, cot_in,
+    act, codes_ref, scales_ref, weight, weight_in, act_in, cot_in,
     other_out, other_in, term_out, term_in,
     load_sem, act_send, act_recv, cot_send, cot_recv,
     w_send, w_recv, s_send, s_recv, g_send, g_recv,
@@ -38,7 +38,8 @@
     loads = [
         pltpu.make_async_copy(there, here, load_sem.at[i])
         for i, (there, here) in enumerate((
-            (codes_hbm, codes_ref), (scales_hbm, scales_ref), (cot_hbm, cot_ref), (act_hbm, act)))
+            (codes_hbm, codes_ref), (scales_hbm, scales_ref),
+            (cot_hbm, cot_in.at[2 * tok : 3 * tok]), (act_hbm, act)))
     ]
     for load in loads:
         load.start()
@@ -58,14 +59,6 @@
     for _, to, _ in line:
         pl.semaphore_signal(barrier, inc=1, device_id=(node, to), device_id_type=MESH)
 
-    loads[0].wait()
-    loads[1].wait()
-    for b in range(blocks):
-        part = codes_ref[b].astype(F32) * scales_ref[b : b + 1, :]
-        weight[b * block : (b + 1) * block, :] = part.astype(BF16)
-    loads[2].wait()
-    cot_in[2 * tok : 3 * tok, :] = cot_ref[...]
-    loads[3].wait()
     pl.semaphore_wait(barrier, len(near) + len(line))
 
     def send(src, dst, send_sem, recv_sem, to_node, to_local):
@@ -73,9 +66,17 @@
             src_ref=src, dst_ref=dst, send_sem=send_sem, recv_sem=recv_sem,
             device_id=(to_node, to_local), device_id_type=MESH)
 
+    def cot_copy(i, source, slot, to):
+        return send(source, cot_in.at[slot * tok : (slot + 1) * tok],
+                    cot_send.at[i], cot_recv.at[i], to, z)
+
     cot_copies = [
-        send(cot_ref, cot_in.at[slot * tok : (slot + 1) * tok], cot_send.at[i], cot_recv.at[i], to, z)
-        for i, (to, slot) in enumerate(zip(near, (3, 0, 1, 4, 5)))
+        cot_copy(i, cot_hbm, slot, to)
+        for i, (to, slot) in enumerate(((along_x[0], 0), (along_y[0], 4), (partner, 3)))
+    ]
+    cot_passes = [
+        cot_copy(3 + i, cot_in.at[slot * tok : (slot + 1) * tok], slot + 1, partner)
+        for i, slot in enumerate((0, 4))
     ]
 
     def column_of(k, owner):
@@ -99,7 +100,7 @@
             to = at(to_y, to_x, to_core)
             for which, owner in ((1, second_of(k, to_y, to_x, to_core)), (0, to)):
                 copies.append(send(
-                    act.at[:, column_of(k, owner)],
+                    (act_hbm if k < 2 else act).at[:, column_of(k, owner)],
                     act_in.at[k, which, row * tok : (row + 1) * tok],
                     act_send.at[k, 2 * i + which], act_recv.at[k, 2 * i + which], to, z))
         return copies
@@ -139,8 +140,16 @@
     for k in range(min(2, n_local)):
         for copy in act_copies(k):
             copy.start()
+
+    loads[0].wait()
+    loads[1].wait()
+    for b in range(blocks):
+        part = codes_ref[b].astype(F32) * scales_ref[b : b + 1, :]
+        weight[b * block : (b + 1) * block, :] = part.astype(BF16)
     for k, to, _ in line:
         line_copy(k, to).start()
+    for load in loads[2:]:
+        load.wait()
 
     def projected(owner, stored):
         return jnp.dot(act[:, pl.ds(aligned(owner, rows), rows)], stored, preferred_element_type=F32)
@@ -154,13 +163,18 @@
         act_in[k, 1, own, :] = act[:, column_of(k, second_of(k, y, x, core))]
         act_in[k, 0, own, :] = act[:, column_of(k, node)]
         if k == 0:
-            for copy in cot_copies:
+            for i, copy in enumerate(cot_copies):
                 copy.wait_recv()
+                if i < 2:
+                    cot_passes[i].start()
+            if n_local > 2:
+                for copy in act_copies(2):
+                    copy.start()
         for copy in act_copies(k):
             copy.wait_recv()
-        if k + 2 < n_local:
-            for copy in act_copies(k + 2):
-                copy.start()
+        if k == 0:
+            for copy in cot_passes:
+                copy.wait_recv()
         cot = cot_in[0 : 4 * tok, :] if over_x else cot_in[2 * tok : 6 * tok, :]
 
         def product(which):
@@ -169,6 +183,9 @@
 
         other_out[k] = product(1)
         sum_copy(k).start()
+        if k + 3 < n_local:
+            for copy in act_copies(k + 3):
+                copy.start()
         term_out[k] = product(0)
 
     def finish_term(k):
@@ -206,7 +223,7 @@
         grad += term_in[k]
     grad_ref[...] = grad * norm
 
-    for copy in cot_copies:
+    for copy in cot_copies + cot_passes:
         copy.wait_send()
     for k in range(n_local):
         for copy in act_copies(k):
@@ -221,6 +238,17 @@
         term_copy(k, to).wait_send()
 
 
+def hand_over_kernel(values, grad, values_out, grad_out, sem):
+    copies = [
+        pltpu.make_async_copy(there, here, sem.at[i])
+        for i, (there, here) in enumerate(((values, values_out), (grad, grad_out)))
+    ]
+    for copy in copies:
+        copy.start()
+    for copy in copies:
+        copy.wait()
+
+
 def exchanged(n_node, n_local, activations, codes, scales, cotangent):
     tok, width = activations.shape
     blocks, block, head = codes.shape
@@ -230,7 +258,7 @@
     vmem = pl.BlockSpec(memory_space=pltpu.VMEM)
     norm = float(tok * n_node * n_local) ** (-0.5)
     piece = pltpu.VMEM((n_local, share, head), F32)
-    return pl.pallas_call(
+    results = pl.pallas_call(
         functools.partial(exchange_kernel, n_local, norm),
         out_shape=(
             jax.ShapeDtypeStruct((tok, head), BF16),
@@ -242,7 +270,6 @@
             pltpu.VMEM((tok, width), BF16),
             pltpu.VMEM(codes.shape, BF16),
             pltpu.VMEM(scales.shape, F32),
-            pltpu.VMEM(cotangent.shape, BF16),
             pltpu.VMEM((rows, head), BF16),
             pltpu.VMEM((n_local - 1, rows, head), BF16),
             pltpu.VMEM((n_local, 2, 4 * tok, share), BF16),
@@ -257,6 +284,14 @@
             flops=4 * tok * width * head, bytes_accessed=2 * tok * width, transcendentals=0
         ),
     )(activations, codes, scales, cotangent)
+    hbm = pl.BlockSpec(memory_space=pltpu.HBM)
+    return pl.pallas_call(
+        hand_over_kernel,
+        out_shape=tuple(jax.ShapeDtypeStruct(r.shape, r.dtype) for r in results),
+        in_specs=[hbm] * 2,
+        out_specs=(hbm, hbm),
+        scratch_shapes=[dma((2,))],
+    )(*results)
 
 
 def gathered(n_node, n_local, activations, codes, scales, cotangent):

time: 28.9 us -> 30.8 us (1.066)
  Pallas kernels: 26 us -> 30.1 us
  local copies, waits for them, and re-layouts: 2.04 us -> 0 us
    pallas_call x0 -> x1, Pallas kernels: none -> 4.1 us  [exchanged(): pl.pallas_call(hand_over_kernel, out_shape=tuple((jax.ShapeDtypeStruct(r....]
    unnamed x4 -> x0, local copies, waits for them, and re-layouts: 2.04 us -> none
where the time goes in v4:
time: 30.8 us; the launch traced here: 30.7 us
  Pallas kernels  30.1 us (98%)
  between operations  0.64 us (2%)
    pallas_call x1, Pallas kernels, exchanged(): pl.pallas_call(functools.partial(exchange_kernel, n_local, norm), out_sha...  26 us
    pallas_call x1, Pallas kernels, exchanged(): pl.pallas_call(hand_over_kernel, out_shape=tuple((jax.ShapeDtypeStruct(r....  4.1 us

profile of v4, /device:TPU:0, one launch (start us, length us, event | category | flops | bytes accessed | tf_op | source)
XLA Modules:
  0.0 30.7 jit_solution(2459393959029798141)
XLA Ops:
  0.6 26.0 %shard_map.59 = (bf16[128,128]{1,0:T(8,128)(2,1)}, f32[128,128]{1,0:T(8,128)}) custom-call(bf16[128,4096]{1,0:T(8,128)(2,1)} %act_hbm.1, bf16[4,256,128]{2,1,0:T(8,128)(2,1)} %codes_hbm.1, f32[4,128]{1,0:T(4,128)} %scales_hbm.1, bf16[128,128]{1,0:T(8,128)(2,1)} %cot_hbm.1), custom_call_target="tpu_custom_call" | custom-call | flops 268435456 | bytes 1048576 | tf_op jit(solution)/shard_map/pallas_call | solution.py:261
  26.6 4.1 %shard_map.60 = (bf16[128,128]{1,0:T(8,128)(2,1)}, f32[128,128]{1,0:T(8,128)}) custom-call(bf16[128,128]{1,0:T(8,128)(2,1)} %get-tuple-element.4.values, f32[128,128]{1,0:T(8,128)} %get-tuple-element.5.grad), custom_call_target="tpu_custom_call" | custom-call | tf_op jit(solution)/shard_map/pallas_call | solution.py:288

commit v5 on v4

--- a/solution.py
+++ b/solution.py
@@ -20,15 +20,15 @@
     n_local, norm,
     act_hbm, codes_hbm, scales_hbm, cot_hbm,
     values_ref, grad_ref,
-    act, codes_ref, scales_ref, weight, weight_in, act_in, cot_in,
-    other_out, other_in, term_out, term_in,
+    act, codes_ref, scales_ref, cot_ref, weight, weight_in, act_in, cot_t, cot_in,
+    other_out, other_in, term_out, term_in, total,
     load_sem, act_send, act_recv, cot_send, cot_recv,
     w_send, w_recv, s_send, s_recv, g_send, g_recv,
 ):
     node, z = lax.axis_index("node"), lax.axis_index("local")
     y, x, core = node // 4, (node // 2) % 2, node % 2
     tok = act.shape[0]
-    share = term_in.shape[1]
+    share = grad_ref.shape[0]
     blocks, block, _ = codes_ref.shape
     rows = blocks * block
     quarter = rows // 4
@@ -39,7 +39,7 @@
         pltpu.make_async_copy(there, here, load_sem.at[i])
         for i, (there, here) in enumerate((
             (codes_hbm, codes_ref), (scales_hbm, scales_ref),
-            (cot_hbm, cot_in.at[2 * tok : 3 * tok]), (act_hbm, act)))
+            (cot_hbm, cot_ref), (act_hbm, act)))
     ]
     for load in loads:
         load.start()
@@ -67,15 +67,15 @@
             device_id=(to_node, to_local), device_id_type=MESH)
 
     def cot_copy(i, source, slot, to):
-        return send(source, cot_in.at[slot * tok : (slot + 1) * tok],
+        return send(source, cot_in.at[:, slot * tok : (slot + 1) * tok],
                     cot_send.at[i], cot_recv.at[i], to, z)
 
     cot_copies = [
-        cot_copy(i, cot_hbm, slot, to)
+        cot_copy(i, cot_t, slot, to)
         for i, (to, slot) in enumerate(((along_x[0], 0), (along_y[0], 4), (partner, 3)))
     ]
     cot_passes = [
-        cot_copy(3 + i, cot_in.at[slot * tok : (slot + 1) * tok], slot + 1, partner)
+        cot_copy(3 + i, cot_in.at[:, slot * tok : (slot + 1) * tok], slot + 1, partner)
         for i, slot in enumerate((0, 4))
     ]
 
@@ -101,7 +101,7 @@
             for which, owner in ((1, second_of(k, to_y, to_x, to_core)), (0, to)):
                 copies.append(send(
                     (act_hbm if k < 2 else act).at[:, column_of(k, owner)],
-                    act_in.at[k, which, row * tok : (row + 1) * tok],
+                    act_in.at[k, row * tok : (row + 1) * tok, which * share : (which + 1) * share],
                     act_send.at[k, 2 * i + which], act_recv.at[k, 2 * i + which], to, z))
         return copies
 
@@ -135,12 +135,12 @@
         return send(weight_in.at[k, part], weight_in.at[k, part],
                     w_send.at[3 + i, k], w_recv.at[3 + i, k], partner, z)
 
+    for copy in act_copies(0):
+        copy.start()
+    loads[2].wait()
+    cot_t[...] = cot_ref[...].T
     for copy in cot_copies:
         copy.start()
-    for k in range(min(2, n_local)):
-        for copy in act_copies(k):
-            copy.start()
-
     loads[0].wait()
     loads[1].wait()
     for b in range(blocks):
@@ -148,20 +148,22 @@
         weight[b * block : (b + 1) * block, :] = part.astype(BF16)
     for k, to, _ in line:
         line_copy(k, to).start()
-    for load in loads[2:]:
-        load.wait()
+    for copy in act_copies(1):
+        copy.start()
+    cot_in[:, 2 * tok : 3 * tok] = cot_t[...]
+    loads[3].wait()
 
     def projected(owner, stored):
         return jnp.dot(act[:, pl.ds(aligned(owner, rows), rows)], stored, preferred_element_type=F32)
 
-    total = projected(z, weight[...])
+    total[...] = projected(z, weight[...])
 
     def group_term(k):
         over_x = k % 2 == 0
         own_row = 2 if over_x else 0
         own = slice(own_row * tok, (own_row + 1) * tok)
-        act_in[k, 1, own, :] = act[:, column_of(k, second_of(k, y, x, core))]
-        act_in[k, 0, own, :] = act[:, column_of(k, node)]
+        act_in[k, own, share : 2 * share] = act[:, column_of(k, second_of(k, y, x, core))]
+        act_in[k, own, 0:share] = act[:, column_of(k, node)]
         if k == 0:
             for i, copy in enumerate(cot_copies):
                 copy.wait_recv()
@@ -175,18 +177,14 @@
         if k == 0:
             for copy in cot_passes:
                 copy.wait_recv()
-        cot = cot_in[0 : 4 * tok, :] if over_x else cot_in[2 * tok : 6 * tok, :]
-
-        def product(which):
-            return lax.dot_general(act_in[k, which], cot, (((0,), (0,)), ((), ())),
-                                   preferred_element_type=F32)
-
-        other_out[k] = product(1)
+        cot = cot_in[:, 0 : 4 * tok] if over_x else cot_in[:, 2 * tok : 6 * tok]
+        both = jnp.dot(cot, act_in[k], preferred_element_type=F32)
+        other_out[k] = both[:, share:]
         sum_copy(k).start()
         if k + 3 < n_local:
             for copy in act_copies(k + 3):
                 copy.start()
-        term_out[k] = product(0)
+        term_out[k] = both[:, :share]
 
     def finish_term(k):
         sum_copy(k).wait_recv()
@@ -215,13 +213,17 @@
     for k, _, owner in line:
         pass_copy(k, 0, parity, 1 - core).wait_recv()
         pass_copy(k, 1, 1 - parity, 1 - core).wait_recv()
-        total += projected(owner, weight_in[k])
-    values_ref[...] = total.astype(BF16)
+    def add_owner(k, _):
+        total[...] += projected(lax.rem(z + last - k, n_local), weight_in[k])
+        return 0
+
+    lax.fori_loop(0, last, add_owner, 0)
+    values_ref[...] = total[...].astype(BF16)
     grad = term_out[last]
     for k, to, _ in line:
         term_copy(k, to).wait_recv()
         grad += term_in[k]
-    grad_ref[...] = grad * norm
+    grad_ref[...] = grad.T * norm
 
     for copy in cot_copies + cot_passes:
         copy.wait_send()
@@ -238,17 +240,6 @@
         term_copy(k, to).wait_send()
 
 
-def hand_over_kernel(values, grad, values_out, grad_out, sem):
-    copies = [
-        pltpu.make_async_copy(there, here, sem.at[i])
-        for i, (there, here) in enumerate(((values, values_out), (grad, grad_out)))
-    ]
-    for copy in copies:
-        copy.start()
-    for copy in copies:
-        copy.wait()
-
-
 def exchanged(n_node, n_local, activations, codes, scales, cotangent):
     tok, width = activations.shape
     blocks, block, head = codes.shape
@@ -257,8 +248,8 @@
     dma = pltpu.SemaphoreType.DMA
     vmem = pl.BlockSpec(memory_space=pltpu.VMEM)
     norm = float(tok * n_node * n_local) ** (-0.5)
-    piece = pltpu.VMEM((n_local, share, head), F32)
-    results = pl.pallas_call(
+    piece = pltpu.VMEM((n_local, head, share), F32)
+    return pl.pallas_call(
         functools.partial(exchange_kernel, n_local, norm),
         out_shape=(
             jax.ShapeDtypeStruct((tok, head), BF16),
@@ -270,11 +261,14 @@
             pltpu.VMEM((tok, width), BF16),
             pltpu.VMEM(codes.shape, BF16),
             pltpu.VMEM(scales.shape, F32),
+            pltpu.VMEM(cotangent.shape, BF16),
             pltpu.VMEM((rows, head), BF16),
             pltpu.VMEM((n_local - 1, rows, head), BF16),
-            pltpu.VMEM((n_local, 2, 4 * tok, share), BF16),
-            pltpu.VMEM((6 * tok, head), BF16),
+            pltpu.VMEM((n_local, 4 * tok, 2 * share), BF16),
+            pltpu.VMEM((head, tok), BF16),
+            pltpu.VMEM((head, 6 * tok), BF16),
             piece, piece, piece, piece,
+            pltpu.VMEM((tok, head), F32),
             dma((4,)), dma((n_local, 6)), dma((n_local, 6)), dma((5,)), dma((5,)),
             dma((5, n_local)), dma((5, n_local)), dma((n_local,)), dma((n_local,)),
             dma((n_local,)), dma((n_local,)),
@@ -284,14 +278,6 @@
             flops=4 * tok * width * head, bytes_accessed=2 * tok * width, transcendentals=0
         ),
     )(activations, codes, scales, cotangent)
-    hbm = pl.BlockSpec(memory_space=pltpu.HBM)
-    return pl.pallas_call(
-        hand_over_kernel,
-        out_shape=tuple(jax.ShapeDtypeStruct(r.shape, r.dtype) for r in results),
-        in_specs=[hbm] * 2,
-        out_specs=(hbm, hbm),
-        scratch_shapes=[dma((2,))],
-    )(*results)
 
 
 def gathered(n_node, n_local, activations, codes, scales, cotangent):
@@ -317,7 +303,8 @@
     def on_device(activations, codes, scales, cotangent):
         share = activations.shape[1] // (n_node * n_local)
         rows = codes.shape[0] * codes.shape[1]
-        fits = n_node == 8 and n_local > 1 and share % 128 == 0 and rows % 128 == 0
+        tok = activations.shape[0]
+        fits = n_node == 8 and n_local > 1 and share % 128 == 0 and rows % 128 == 0 and tok % 128 == 0
         run = exchanged if fits else gathered
         return run(n_node, n_local, activations, codes, scales, cotangent)
 

time: 30.8 us -> 29.4 us (0.955)
  Pallas kernels: 30.1 us -> 26.5 us
  local copies, waits for them, and re-layouts: 0 us -> 2.04 us
    pallas_call x1 -> x0, Pallas kernels: 4.1 us -> none  [exchanged(): pl.pallas_call(hand_over_kernel, out_shape=tuple((jax.ShapeDtypeStruct(r....]
    unnamed x0 -> x4, local copies, waits for them, and re-layouts: none -> 2.04 us
    pallas_call x1, Pallas kernels: 26 us -> 26.5 us  [exchanged(): pl.pallas_call(functools.partial(exchange_kernel, n_local, norm), out_sha...]
where the time goes in v5:
time: 29.4 us; the launch traced here: 29.2 us
  Pallas kernels  26.5 us (90%)
  local copies, waits for them, and re-layouts  2.04 us (7%)
  between operations  0.65 us (2%)
    pallas_call x1, Pallas kernels, exchanged(): pl.pallas_call(functools.partial(exchange_kernel, n_local, norm), out_sha...  26.5 us
    unnamed x4, local copies, waits for them, and re-layouts  2.04 us

profile of v5, /device:TPU:0, one launch (start us, length us, event | category | flops | bytes accessed | tf_op | source)
XLA Modules:
  0.0 29.2 jit_solution(8481192860769498108)
XLA Ops:
  0.6 26.5 %shard_map.59 = (bf16[128,128]{1,0:T(8,128)(2,1)}, f32[128,128]{1,0:T(8,128)}) custom-call(bf16[128,4096]{1,0:T(8,128)(2,1)} %act_hbm.1, bf16[4,256,128]{2,1,0:T(8,128)(2,1)} %codes_hbm.1, f32[4,128]{1,0:T(4,128)} %scales_hbm.1, bf16[128,128]{1,0:T(8,128)(2,1)} %cot_hbm.1), custom_call_target="tpu_custom_call" | custom-call | flops 268435456 | bytes 1048576 | tf_op jit(solution)/shard_map/pallas_call | solution.py:252
  27.2 0.0 copy-start
  27.2 1.4 %copy.8 = bf16[128,128]{1,0:T(8,128)(2,1)} copy(bf16[128,128]{1,0:T(8,128)(2,1)} %get-tuple-element.4) | data formatting | bytes 65536
  28.6 0.0 copy-done
  28.6 0.6 %copy.9 = f32[128,128]{1,0:T(8,128)} copy(f32[128,128]{1,0:T(8,128)S(1)} %copy-done) | data formatting | bytes 131072
Async XLA Ops:
  27.2 1.4 %copy-start = (f32[128,128]{1,0:T(8,128)S(1)}, f32[128,128]{1,0:T(8,128)}, u32[]{:S(2)}) copy-start(f32[128,128]{1,0:T(8,128)} %get-tuple-element.5) | copy-start | bytes 196612

commit v6 on v5

--- a/solution.py
+++ b/solution.py
@@ -23,7 +23,7 @@
     act, codes_ref, scales_ref, cot_ref, weight, weight_in, act_in, cot_t, cot_in,
     other_out, other_in, term_out, term_in, total,
     load_sem, act_send, act_recv, cot_send, cot_recv,
-    w_send, w_recv, s_send, s_recv, g_send, g_recv,
+    line_send, line_recv, w_send, w_recv, s_send, s_recv, g_send, g_recv,
 ):
     node, z = lax.axis_index("node"), lax.axis_index("local")
     y, x, core = node // 4, (node // 2) % 2, node % 2
@@ -102,8 +102,12 @@
                 copies.append(send(
                     (act_hbm if k < 2 else act).at[:, column_of(k, owner)],
                     act_in.at[k, row * tok : (row + 1) * tok, which * share : (which + 1) * share],
-                    act_send.at[k, 2 * i + which], act_recv.at[k, 2 * i + which], to, z))
+                    act_send.at[k], act_recv.at[k], to, z))
         return copies
+
+    def act_whole(k):
+        ref = act_in.at[k, 0 : 3 * tok]
+        return send(ref, ref, act_send.at[k], act_recv.at[k], partner, z)
 
     def sum_copy(k):
         return send(other_out.at[k], other_in.at[k], s_send.at[k], s_recv.at[k],
@@ -119,21 +123,24 @@
 
     def line_copy(k, to):
         part = part_of(parity, core, 0, 2)
-        return send(weight.at[part], weight_in.at[k, part], w_send.at[0, k], w_recv.at[0, k], node, to)
-
-    def plane_copies(k, of_parity):
+        return send(weight.at[part], weight_in.at[k, part], line_send, line_recv, node, to)
+
+    def line_whole():
+        ref = weight_in.at[:, part_of(parity, core, 0, 2)]
+        return send(ref, ref, line_send, line_recv, partner, z)
+
+    def owners_copy(i, to, part):
+        ref = weight_in.at[:, part]
+        return send(ref, ref, w_send.at[i], w_recv.at[i], to, z)
+
+    def plane_copies(of_parity):
         return [
-            send(weight_in.at[k, part], weight_in.at[k, part],
-                 w_send.at[1 + i, k], w_recv.at[1 + i, k], to, z)
-            for i, (to, part) in enumerate((
-                (along_x[0], part_of(of_parity, core, 0, 1)),
-                (along_y[0], part_of(of_parity, core, 1, 1))))
+            owners_copy(0, along_x[0], part_of(of_parity, core, 0, 1)),
+            owners_copy(1, along_y[0], part_of(of_parity, core, 1, 1)),
         ]
 
-    def pass_copy(k, i, of_parity, of_core):
-        part = part_of(of_parity, of_core, 0, 2)
-        return send(weight_in.at[k, part], weight_in.at[k, part],
-                    w_send.at[3 + i, k], w_recv.at[3 + i, k], partner, z)
+    def pass_copy(i, of_parity, of_core):
+        return owners_copy(2 + i, partner, part_of(of_parity, of_core, 0, 2))
 
     for copy in act_copies(0):
         copy.start()
@@ -172,8 +179,7 @@
             if n_local > 2:
                 for copy in act_copies(2):
                     copy.start()
-        for copy in act_copies(k):
-            copy.wait_recv()
+        act_whole(k).wait_recv()
         if k == 0:
             for copy in cot_passes:
                 copy.wait_recv()
@@ -192,51 +198,42 @@
         if k < last:
             term_copy(k, line[k][1]).start()
 
-    early = min(2, n_local)
-    for k in range(early):
-        group_term(k)
-    for k, to, _ in line:
-        line_copy(k, to).wait_recv()
-        for copy in plane_copies(k, parity):
-            copy.start()
-        pass_copy(k, 0, parity, core).start()
-    for k in range(early):
-        finish_term(k)
-    for k in range(early, n_local):
-        group_term(k)
-    for k, _, _ in line:
-        for copy in plane_copies(k, 1 - parity):
-            copy.wait_recv()
-        pass_copy(k, 1, 1 - parity, core).start()
-    for k in range(early, n_local):
-        finish_term(k)
-    for k, _, owner in line:
-        pass_copy(k, 0, parity, 1 - core).wait_recv()
-        pass_copy(k, 1, 1 - parity, 1 - core).wait_recv()
     def add_owner(k, _):
         total[...] += projected(lax.rem(z + last - k, n_local), weight_in[k])
         return 0
 
+    for k in range(n_local):
+        group_term(k)
+        if k == 0:
+            line_whole().wait_recv()
+            for copy in plane_copies(parity):
+                copy.start()
+            pass_copy(0, parity, core).start()
+        else:
+            finish_term(k - 1)
+    for copy in plane_copies(1 - parity):
+        copy.wait_recv()
+    pass_copy(1, 1 - parity, core).start()
+    for copy in cot_copies + cot_passes + plane_copies(parity):
+        copy.wait_send()
+    for k in range(n_local):
+        act_whole(k).wait_send()
+    line_whole().wait_send()
+    pass_copy(0, parity, core).wait_send()
+    pass_copy(0, parity, 1 - core).wait_recv()
+    pass_copy(1, 1 - parity, 1 - core).wait_recv()
     lax.fori_loop(0, last, add_owner, 0)
     values_ref[...] = total[...].astype(BF16)
+    finish_term(last)
+    pass_copy(1, 1 - parity, core).wait_send()
+    for k in range(n_local):
+        sum_copy(k).wait_send()
     grad = term_out[last]
     for k, to, _ in line:
         term_copy(k, to).wait_recv()
         grad += term_in[k]
     grad_ref[...] = grad.T * norm
-
-    for copy in cot_copies + cot_passes:
-        copy.wait_send()
-    for k in range(n_local):
-        for copy in act_copies(k):
-            copy.wait_send()
-        sum_copy(k).wait_send()
     for k, to, _ in line:
-        line_copy(k, to).wait_send()
-        for copy in plane_copies(k, parity):
-            copy.wait_send()
-        pass_copy(k, 0, parity, core).wait_send()
-        pass_copy(k, 1, 1 - parity, core).wait_send()
         term_copy(k, to).wait_send()
 
 
@@ -269,8 +266,8 @@
             pltpu.VMEM((head, 6 * tok), BF16),
             piece, piece, piece, piece,
             pltpu.VMEM((tok, head), F32),
-            dma((4,)), dma((n_local, 6)), dma((n_local, 6)), dma((5,)), dma((5,)),
-            dma((5, n_local)), dma((5, n_local)), dma((n_local,)), dma((n_local,)),
+            dma((4,)), dma((n_local,)), dma((n_local,)), dma((5,)), dma((5,)),
+            dma, dma, dma((4,)), dma((4,)), dma((n_local,)), dma((n_local,)),
             dma((n_local,)), dma((n_local,)),
         ],
         compiler_params=pltpu.CompilerParams(collective_id=0, has_side_effects=True),

time: 29.4 us -> 28.7 us (0.976)
  Pallas kernels: 26.5 us -> 25.9 us
    pallas_call x1, Pallas kernels: 26.5 us -> 25.9 us  [exchanged(): pl.pallas_call(functools.partial(exchange_kernel, n_local, norm), out_sha...]
where the time goes in v6:
time: 28.7 us; the launch traced here: 28.6 us
  Pallas kernels  25.9 us (90%)
  local copies, waits for them, and re-layouts  2.04 us (7%)
  between operations  0.65 us (2%)
    pallas_call x1, Pallas kernels, exchanged(): pl.pallas_call(functools.partial(exchange_kernel, n_local, norm), out_sha...  25.9 us
    unnamed x4, local copies, waits for them, and re-layouts  2.04 us

profile of v6, /device:TPU:0, one launch (start us, length us, event | category | flops | bytes accessed | tf_op | source)
XLA Modules:
  0.0 28.6 jit_solution(13724932888269285614)
XLA Ops:
  0.6 25.9 %shard_map.59 = (bf16[128,128]{1,0:T(8,128)(2,1)}, f32[128,128]{1,0:T(8,128)}) custom-call(bf16[128,4096]{1,0:T(8,128)(2,1)} %act_hbm.1, bf16[4,256,128]{2,1,0:T(8,128)(2,1)} %codes_hbm.1, f32[4,128]{1,0:T(4,128)} %scales_hbm.1, bf16[128,128]{1,0:T(8,128)(2,1)} %cot_hbm.1), custom_call_target="tpu_custom_call" | custom-call | flops 268435456 | bytes 1048576 | tf_op jit(solution)/shard_map/pallas_call | solution.py:249
  26.5 0.0 copy-start
  26.5 1.4 %copy.8 = bf16[128,128]{1,0:T(8,128)(2,1)} copy(bf16[128,128]{1,0:T(8,128)(2,1)} %get-tuple-element.4) | data formatting | bytes 65536
  27.9 0.0 copy-done
  27.9 0.6 %copy.9 = f32[128,128]{1,0:T(8,128)} copy(f32[128,128]{1,0:T(8,128)S(1)} %copy-done) | data formatting | bytes 131072
Async XLA Ops:
  26.5 1.4 %copy-start = (f32[128,128]{1,0:T(8,128)S(1)}, f32[128,128]{1,0:T(8,128)}, u32[]{:S(2)}) copy-start(f32[128,128]{1,0:T(8,128)} %get-tuple-element.5) | copy-start | bytes 196612

commit v7 on v6

--- a/solution.py
+++ b/solution.py
@@ -20,7 +20,7 @@
     n_local, norm,
     act_hbm, codes_hbm, scales_hbm, cot_hbm,
     values_ref, grad_ref,
-    act, codes_ref, scales_ref, cot_ref, weight, weight_in, act_in, cot_t, cot_in,
+    act, act_parts, codes_ref, scales_ref, cot_ref, weight, weight_in, act_in, cot_t, cot_in,
     other_out, other_in, term_out, term_in, total,
     load_sem, act_send, act_recv, cot_send, cot_recv,
     line_send, line_recv, w_send, w_recv, s_send, s_recv, g_send, g_recv,
@@ -67,7 +67,7 @@
             device_id=(to_node, to_local), device_id_type=MESH)
 
     def cot_copy(i, source, slot, to):
-        return send(source, cot_in.at[:, slot * tok : (slot + 1) * tok],
+        return send(source, cot_in.at[slot],
                     cot_send.at[i], cot_recv.at[i], to, z)
 
     cot_copies = [
@@ -75,43 +75,40 @@
         for i, (to, slot) in enumerate(((along_x[0], 0), (along_y[0], 4), (partner, 3)))
     ]
     cot_passes = [
-        cot_copy(3 + i, cot_in.at[:, slot * tok : (slot + 1) * tok], slot + 1, partner)
+        cot_copy(3 + i, cot_in.at[slot], slot + 1, partner)
         for i, slot in enumerate((0, 4))
     ]
 
-    def column_of(k, owner):
-        return pl.ds(aligned(owner * n_local + (z + 1 + k) % n_local, share), share)
-
-    def second_of(k, owner_y, owner_x, owner_core):
+    def second_of(k):
+        return at(1 - y, x, core) if k % 2 == 0 else at(y, 1 - x, core)
+
+    def chunks_of(k, to_y, to_x, to_core):
+        owner = (z + 1 + k) % n_local
         if k % 2 == 0:
-            return at(1 - owner_y, owner_x, owner_core)
-        return at(owner_y, 1 - owner_x, owner_core)
+            return act_parts.at[:, to_x, to_core, owner]
+        return act_parts.at[to_y, :, to_core, owner]
 
     def act_copies(k):
         over_x = k % 2 == 0
         first = (y, 1 - x) if over_x else (1 - y, x)
         own_row, first_row = (2, 0) if over_x else (0, 2)
-        copies = []
-        for i, (to_y, to_x, to_core, row) in enumerate((
-            (first[0], first[1], core, first_row),
-            (first[0], first[1], 1 - core, first_row + 1),
-            (y, x, 1 - core, own_row + 1),
-        )):
-            to = at(to_y, to_x, to_core)
-            for which, owner in ((1, second_of(k, to_y, to_x, to_core)), (0, to)):
-                copies.append(send(
-                    (act_hbm if k < 2 else act).at[:, column_of(k, owner)],
-                    act_in.at[k, row * tok : (row + 1) * tok, which * share : (which + 1) * share],
-                    act_send.at[k], act_recv.at[k], to, z))
-        return copies
+        return [
+            send(chunks_of(k, to_y, to_x, to_core),
+                 act_in.at[k, :, row * tok : (row + 1) * tok],
+                 act_send.at[k], act_recv.at[k], at(to_y, to_x, to_core), z)
+            for to_y, to_x, to_core, row in (
+                (first[0], first[1], core, first_row),
+                (first[0], first[1], 1 - core, first_row + 1),
+                (y, x, 1 - core, own_row + 1))
+        ]
 
     def act_whole(k):
-        ref = act_in.at[k, 0 : 3 * tok]
+        ref = act_in.at[k, :, 0 : 3 * tok]
         return send(ref, ref, act_send.at[k], act_recv.at[k], partner, z)
 
     def sum_copy(k):
         return send(other_out.at[k], other_in.at[k], s_send.at[k], s_recv.at[k],
-                    second_of(k, y, x, core), z)
+                    second_of(k), z)
 
     def term_copy(k, to):
         return send(term_out.at[k], term_in.at[k], g_send.at[k], g_recv.at[k], node, to)
@@ -142,6 +139,11 @@
     def pass_copy(i, of_parity, of_core):
         return owners_copy(2 + i, partner, part_of(of_parity, of_core, 0, 2))
 
+    loads[3].wait()
+    for i in range(8):
+        for j in range(n_local):
+            column = (i * n_local + j) * share
+            act_parts[i // 4, (i // 2) % 2, i % 2, j] = act[:, column : column + share]
     for copy in act_copies(0):
         copy.start()
     loads[2].wait()
@@ -157,8 +159,7 @@
         line_copy(k, to).start()
     for copy in act_copies(1):
         copy.start()
-    cot_in[:, 2 * tok : 3 * tok] = cot_t[...]
-    loads[3].wait()
+    cot_in[2] = cot_t[...]
 
     def projected(owner, stored):
         return jnp.dot(act[:, pl.ds(aligned(owner, rows), rows)], stored, preferred_element_type=F32)
@@ -169,8 +170,7 @@
         over_x = k % 2 == 0
         own_row = 2 if over_x else 0
         own = slice(own_row * tok, (own_row + 1) * tok)
-        act_in[k, own, share : 2 * share] = act[:, column_of(k, second_of(k, y, x, core))]
-        act_in[k, own, 0:share] = act[:, column_of(k, node)]
+        act_in[k, :, own, :] = chunks_of(k, y, x, core)[...]
         if k == 0:
             for i, copy in enumerate(cot_copies):
                 copy.wait_recv()
@@ -183,14 +183,15 @@
         if k == 0:
             for copy in cot_passes:
                 copy.wait_recv()
-        cot = cot_in[:, 0 : 4 * tok] if over_x else cot_in[:, 2 * tok : 6 * tok]
-        both = jnp.dot(cot, act_in[k], preferred_element_type=F32)
-        other_out[k] = both[:, share:]
+        begin = 0 if over_x else 2
+        mine = y if over_x else x
+        cot = jnp.concatenate([cot_in[begin + i] for i in range(4)], axis=1)
+        other_out[k] = jnp.dot(cot, act_in[k, 1 - mine], preferred_element_type=F32)
         sum_copy(k).start()
         if k + 3 < n_local:
             for copy in act_copies(k + 3):
                 copy.start()
-        term_out[k] = both[:, :share]
+        term_out[k] = jnp.dot(cot, act_in[k, mine], preferred_element_type=F32)
 
     def finish_term(k):
         sum_copy(k).wait_recv()
@@ -256,14 +257,15 @@
         out_specs=(vmem, vmem),
         scratch_shapes=[
             pltpu.VMEM((tok, width), BF16),
+            pltpu.VMEM((2, 2, 2, n_local, tok, share), BF16),
             pltpu.VMEM(codes.shape, BF16),
             pltpu.VMEM(scales.shape, F32),
             pltpu.VMEM(cotangent.shape, BF16),
             pltpu.VMEM((rows, head), BF16),
             pltpu.VMEM((n_local - 1, rows, head), BF16),
-            pltpu.VMEM((n_local, 4 * tok, 2 * share), BF16),
+            pltpu.VMEM((n_local, 2, 4 * tok, share), BF16),
             pltpu.VMEM((head, tok), BF16),
-            pltpu.VMEM((head, 6 * tok), BF16),
+            pltpu.VMEM((6, head, tok), BF16),
             piece, piece, piece, piece,
             pltpu.VMEM((tok, head), F32),
             dma((4,)), dma((n_local,)), dma((n_local,)), dma((5,)), dma((5,)),

time: 28.7 us -> 28.6 us (level)
  no operation moved by 1% of the time
where the time goes in v7:
time: 28.6 us; the launch traced here: 28.4 us
  Pallas kernels  25.8 us (90%)
  local copies, waits for them, and re-layouts  2.04 us (7%)
  between operations  0.65 us (2%)
    pallas_call x1, Pallas kernels, exchanged(): pl.pallas_call(functools.partial(exchange_kernel, n_local, norm), out_sha...  25.8 us
    unnamed x4, local copies, waits for them, and re-layouts  2.04 us

profile of v7, /device:TPU:0, one launch (start us, length us, event | category | flops | bytes accessed | tf_op | source)
XLA Modules:
  0.0 28.4 jit_solution(16506642571581370672)
XLA Ops:
  0.6 25.8 %shard_map.59 = (bf16[128,128]{1,0:T(8,128)(2,1)}, f32[128,128]{1,0:T(8,128)}) custom-call(bf16[128,4096]{1,0:T(8,128)(2,1)} %act_hbm.1, bf16[4,256,128]{2,1,0:T(8,128)(2,1)} %codes_hbm.1, f32[4,128]{1,0:T(4,128)} %scales_hbm.1, bf16[128,128]{1,0:T(8,128)(2,1)} %cot_hbm.1), custom_call_target="tpu_custom_call" | custom-call | flops 268435456 | bytes 1048576 | tf_op jit(solution)/shard_map/pallas_call | solution.py:250
  26.4 0.0 copy-start
  26.4 1.4 %copy.8 = bf16[128,128]{1,0:T(8,128)(2,1)} copy(bf16[128,128]{1,0:T(8,128)(2,1)} %get-tuple-element.4) | data formatting | bytes 65536
  27.8 0.0 copy-done
  27.8 0.6 %copy.9 = f32[128,128]{1,0:T(8,128)} copy(f32[128,128]{1,0:T(8,128)S(1)} %copy-done) | data formatting | bytes 131072
Async XLA Ops:
  26.4 1.4 %copy-start = (f32[128,128]{1,0:T(8,128)S(1)}, f32[128,128]{1,0:T(8,128)}, u32[]{:S(2)}) copy-start(f32[128,128]{1,0:T(8,128)} %get-tuple-element.5) | copy-start | bytes 196612

commit v8 on v7

--- a/solution.py
+++ b/solution.py
@@ -82,6 +82,9 @@
     def second_of(k):
         return at(1 - y, x, core) if k % 2 == 0 else at(y, 1 - x, core)
 
+    def column_of(k, owner):
+        return pl.ds(aligned(owner * n_local + (z + 1 + k) % n_local, share), share)
+
     def chunks_of(k, to_y, to_x, to_core):
         owner = (z + 1 + k) % n_local
         if k % 2 == 0:
@@ -92,15 +95,25 @@
         over_x = k % 2 == 0
         first = (y, 1 - x) if over_x else (1 - y, x)
         own_row, first_row = (2, 0) if over_x else (0, 2)
-        return [
-            send(chunks_of(k, to_y, to_x, to_core),
-                 act_in.at[k, :, row * tok : (row + 1) * tok],
-                 act_send.at[k], act_recv.at[k], at(to_y, to_x, to_core), z)
-            for to_y, to_x, to_core, row in (
-                (first[0], first[1], core, first_row),
-                (first[0], first[1], 1 - core, first_row + 1),
-                (y, x, 1 - core, own_row + 1))
-        ]
+        copies = []
+        for to_y, to_x, to_core, row in (
+            (first[0], first[1], core, first_row),
+            (first[0], first[1], 1 - core, first_row + 1),
+            (y, x, 1 - core, own_row + 1),
+        ):
+            place = pl.ds(row * tok, tok)
+            if k < 2:
+                pairs = [
+                    (act_hbm.at[:, column_of(k, at(i, to_x, to_core) if over_x else at(to_y, i, to_core))],
+                     act_in.at[k, i, place])
+                    for i in range(2)
+                ]
+            else:
+                pairs = [(chunks_of(k, to_y, to_x, to_core), act_in.at[k, :, place])]
+            for src, dst in pairs:
+                copies.append(send(src, dst, act_send.at[k], act_recv.at[k],
+                                   at(to_y, to_x, to_core), z))
+        return copies
 
     def act_whole(k):
         ref = act_in.at[k, :, 0 : 3 * tok]
@@ -139,12 +152,7 @@
     def pass_copy(i, of_parity, of_core):
         return owners_copy(2 + i, partner, part_of(of_parity, of_core, 0, 2))
 
-    loads[3].wait()
-    for i in range(8):
-        for j in range(n_local):
-            column = (i * n_local + j) * share
-            act_parts[i // 4, (i // 2) % 2, i % 2, j] = act[:, column : column + share]
-    for copy in act_copies(0):
+    for copy in act_copies(0) + act_copies(1):
         copy.start()
     loads[2].wait()
     cot_t[...] = cot_ref[...].T
@@ -157,8 +165,11 @@
         weight[b * block : (b + 1) * block, :] = part.astype(BF16)
     for k, to, _ in line:
         line_copy(k, to).start()
-    for copy in act_copies(1):
-        copy.start()
+    loads[3].wait()
+    for i in range(8):
+        for j in range(n_local):
+            column = (i * n_local + j) * share
+            act_parts[i // 4, (i // 2) % 2, i % 2, j] = act[:, column : column + share]
     cot_in[2] = cot_t[...]
 
     def projected(owner, stored):
@@ -199,31 +210,45 @@
         if k < last:
             term_copy(k, line[k][1]).start()
 
-    def add_owner(k, _):
-        total[...] += projected(lax.rem(z + last - k, n_local), weight_in[k])
-        return 0
-
-    for k in range(n_local):
+    def add_quarter(of_parity, of_core):
+        begin = (of_parity * 2 + of_core) * quarter
+
+        def add_owner(k, _):
+            column = aligned(lax.rem(z + last - k, n_local) * (rows // quarter)
+                             + of_parity * 2 + of_core, quarter)
+            total[...] += jnp.dot(
+                act[:, pl.ds(column, quarter)],
+                weight_in[k, pl.ds(pl.multiple_of(begin, quarter), quarter)],
+                preferred_element_type=F32)
+            return 0
+
+        lax.fori_loop(0, last, add_owner, 0)
+
+    group_term(0)
+    line_whole().wait_recv()
+    for copy in plane_copies(parity):
+        copy.start()
+    pass_copy(0, parity, core).start()
+    add_quarter(parity, core)
+    for k in range(1, last):
         group_term(k)
-        if k == 0:
-            line_whole().wait_recv()
-            for copy in plane_copies(parity):
-                copy.start()
-            pass_copy(0, parity, core).start()
-        else:
-            finish_term(k - 1)
+        finish_term(k - 1)
+    pass_copy(0, parity, 1 - core).wait_recv()
+    add_quarter(parity, 1 - core)
     for copy in plane_copies(1 - parity):
         copy.wait_recv()
     pass_copy(1, 1 - parity, core).start()
+    finish_term(last - 1)
+    group_term(last)
+    add_quarter(1 - parity, core)
     for copy in cot_copies + cot_passes + plane_copies(parity):
         copy.wait_send()
     for k in range(n_local):
         act_whole(k).wait_send()
     line_whole().wait_send()
     pass_copy(0, parity, core).wait_send()
-    pass_copy(0, parity, 1 - core).wait_recv()
     pass_copy(1, 1 - parity, 1 - core).wait_recv()
-    lax.fori_loop(0, last, add_owner, 0)
+    add_quarter(1 - parity, 1 - core)
     values_ref[...] = total[...].astype(BF16)
     finish_term(last)
     pass_copy(1, 1 - parity, core).wait_send()
@@ -303,7 +328,7 @@
         share = activations.shape[1] // (n_node * n_local)
         rows = codes.shape[0] * codes.shape[1]
         tok = activations.shape[0]
-        fits = n_node == 8 and n_local > 1 and share % 128 == 0 and rows % 128 == 0 and tok % 128 == 0
+        fits = n_node == 8 and n_local > 1 and share % 128 == 0 and rows % 512 == 0 and tok % 128 == 0
         run = exchanged if fits else gathered
         return run(n_node, n_local, activations, codes, scales, cotangent)
 

time: 28.6 us -> 28.9 us (1.010)
  no operation moved by 1% of the time
where the time goes in v8:
time: 28.9 us; the launch traced here: 28.7 us
  Pallas kernels  26 us (90%)
  local copies, waits for them, and re-layouts  2.04 us (7%)
  between operations  0.65 us (2%)
    pallas_call x1, Pallas kernels, exchanged(): pl.pallas_call(functools.partial(exchange_kernel, n_local, norm), out_sha...  26 us
    unnamed x4, local copies, waits for them, and re-layouts  2.04 us

profile of v8, /device:TPU:0, one launch (start us, length us, event | category | flops | bytes accessed | tf_op | source)
XLA Modules:
  0.0 28.7 jit_solution(5872102263587156273)
XLA Ops:
  0.6 26.0 %shard_map.59 = (bf16[128,128]{1,0:T(8,128)(2,1)}, f32[128,128]{1,0:T(8,128)}) custom-call(bf16[128,4096]{1,0:T(8,128)(2,1)} %act_hbm.1, bf16[4,256,128]{2,1,0:T(8,128)(2,1)} %codes_hbm.1, f32[4,128]{1,0:T(4,128)} %scales_hbm.1, bf16[128,128]{1,0:T(8,128)(2,1)} %cot_hbm.1), custom_call_target="tpu_custom_call" | custom-call | flops 268435456 | bytes 1048576 | tf_op jit(solution)/shard_map/pallas_call | solution.py:275
  26.7 0.0 copy-start
  26.7 1.4 %copy.8 = bf16[128,128]{1,0:T(8,128)(2,1)} copy(bf16[128,128]{1,0:T(8,128)(2,1)} %get-tuple-element.4) | data formatting | bytes 65536
  28.1 0.0 copy-done
  28.1 0.6 %copy.9 = f32[128,128]{1,0:T(8,128)} copy(f32[128,128]{1,0:T(8,128)S(1)} %copy-done) | data formatting | bytes 131072
Async XLA Ops:
  26.7 1.4 %copy-start = (f32[128,128]{1,0:T(8,128)S(1)}, f32[128,128]{1,0:T(8,128)}, u32[]{:S(2)}) copy-start(f32[128,128]{1,0:T(8,128)} %get-tuple-element.5) | copy-start | bytes 196612

commit v9 on v8

--- a/solution.py
+++ b/solution.py
@@ -23,7 +23,7 @@
     act, act_parts, codes_ref, scales_ref, cot_ref, weight, weight_in, act_in, cot_t, cot_in,
     other_out, other_in, term_out, term_in, total,
     load_sem, act_send, act_recv, cot_send, cot_recv,
-    line_send, line_recv, w_send, w_recv, s_send, s_recv, g_send, g_recv,
+    w_send, w_recv, f_send, f_recv, s_send, s_recv, g_send, g_recv,
 ):
     node, z = lax.axis_index("node"), lax.axis_index("local")
     y, x, core = node // 4, (node // 2) % 2, node % 2
@@ -31,8 +31,7 @@
     share = grad_ref.shape[0]
     blocks, block, _ = codes_ref.shape
     rows = blocks * block
-    quarter = rows // 4
-    eighth = quarter // 2
+    half = rows // 2
     last = n_local - 1
 
     loads = [
@@ -126,31 +125,16 @@
     def term_copy(k, to):
         return send(term_out.at[k], term_in.at[k], g_send.at[k], g_recv.at[k], node, to)
 
-    parity = (x + y) % 2
-
-    def part_of(of_parity, of_core, begin, size):
-        return pl.ds(aligned((of_parity * 2 + of_core) * 2 + begin, eighth), size * eighth)
+    def half_of(of_core):
+        return pl.ds(aligned(of_core, half), half)
 
     def line_copy(k, to):
-        part = part_of(parity, core, 0, 2)
-        return send(weight.at[part], weight_in.at[k, part], line_send, line_recv, node, to)
-
-    def line_whole():
-        ref = weight_in.at[:, part_of(parity, core, 0, 2)]
-        return send(ref, ref, line_send, line_recv, partner, z)
-
-    def owners_copy(i, to, part):
-        ref = weight_in.at[:, part]
-        return send(ref, ref, w_send.at[i], w_recv.at[i], to, z)
-
-    def plane_copies(of_parity):
-        return [
-            owners_copy(0, along_x[0], part_of(of_parity, core, 0, 1)),
-            owners_copy(1, along_y[0], part_of(of_parity, core, 1, 1)),
-        ]
-
-    def pass_copy(i, of_parity, of_core):
-        return owners_copy(2 + i, partner, part_of(of_parity, of_core, 0, 2))
+        part = half_of(core)
+        return send(weight.at[part], weight_in.at[k, part], w_send.at[k], w_recv.at[k], node, to)
+
+    def pass_copy(k, of_core):
+        ref = weight_in.at[k, half_of(of_core)]
+        return send(ref, ref, f_send.at[k], f_recv.at[k], partner, z)
 
     for copy in act_copies(0) + act_copies(1):
         copy.start()
@@ -210,48 +194,33 @@
         if k < last:
             term_copy(k, line[k][1]).start()
 
-    def add_quarter(of_parity, of_core):
-        begin = (of_parity * 2 + of_core) * quarter
-
-        def add_owner(k, _):
-            column = aligned(lax.rem(z + last - k, n_local) * (rows // quarter)
-                             + of_parity * 2 + of_core, quarter)
-            total[...] += jnp.dot(
-                act[:, pl.ds(column, quarter)],
-                weight_in[k, pl.ds(pl.multiple_of(begin, quarter), quarter)],
-                preferred_element_type=F32)
-            return 0
-
-        lax.fori_loop(0, last, add_owner, 0)
+    def add_half(k, owner, of_core):
+        column = aligned(owner * 2 + of_core, half)
+        total[...] += jnp.dot(act[:, pl.ds(column, half)], weight_in[k, half_of(of_core)],
+                              preferred_element_type=F32)
 
     group_term(0)
-    line_whole().wait_recv()
-    for copy in plane_copies(parity):
-        copy.start()
-    pass_copy(0, parity, core).start()
-    add_quarter(parity, core)
     for k in range(1, last):
         group_term(k)
         finish_term(k - 1)
-    pass_copy(0, parity, 1 - core).wait_recv()
-    add_quarter(parity, 1 - core)
-    for copy in plane_copies(1 - parity):
-        copy.wait_recv()
-    pass_copy(1, 1 - parity, core).start()
+    for k, to, owner in line:
+        line_copy(k, to).wait_recv()
+        pass_copy(k, core).start()
+        add_half(k, owner, core)
     finish_term(last - 1)
     group_term(last)
-    add_quarter(1 - parity, core)
-    for copy in cot_copies + cot_passes + plane_copies(parity):
+    for copy in cot_copies + cot_passes:
         copy.wait_send()
     for k in range(n_local):
         act_whole(k).wait_send()
-    line_whole().wait_send()
-    pass_copy(0, parity, core).wait_send()
-    pass_copy(1, 1 - parity, 1 - core).wait_recv()
-    add_quarter(1 - parity, 1 - core)
+    for k, to, owner in line:
+        line_copy(k, to).wait_send()
+        pass_copy(k, 1 - core).wait_recv()
+        add_half(k, owner, 1 - core)
     values_ref[...] = total[...].astype(BF16)
     finish_term(last)
-    pass_copy(1, 1 - parity, core).wait_send()
+    for k, _, _ in line:
+        pass_copy(k, core).wait_send()
     for k in range(n_local):
         sum_copy(k).wait_send()
     grad = term_out[last]
@@ -294,7 +263,8 @@
             piece, piece, piece, piece,
             pltpu.VMEM((tok, head), F32),
             dma((4,)), dma((n_local,)), dma((n_local,)), dma((5,)), dma((5,)),
-            dma, dma, dma((4,)), dma((4,)), dma((n_local,)), dma((n_local,)),
+            dma((n_local,)), dma((n_local,)), dma((n_local,)), dma((n_local,)),
+            dma((n_local,)), dma((n_local,)),
             dma((n_local,)), dma((n_local,)),
         ],
         compiler_params=pltpu.CompilerParams(collective_id=0, has_side_effects=True),
@@ -328,7 +298,7 @@
         share = activations.shape[1] // (n_node * n_local)
         rows = codes.shape[0] * codes.shape[1]
         tok = activations.shape[0]
-        fits = n_node == 8 and n_local > 1 and share % 128 == 0 and rows % 512 == 0 and tok % 128 == 0
+        fits = n_node == 8 and n_local > 1 and share % 128 == 0 and rows % 256 == 0 and tok % 128 == 0
         run = exchanged if fits else gathered
         return run(n_node, n_local, activations, codes, scales, cotangent)
 

time: 28.9 us -> 28 us (0.969)
  Pallas kernels: 26 us -> 25.2 us
    pallas_call x1, Pallas kernels: 26 us -> 25.2 us  [exchanged(): pl.pallas_call(functools.partial(exchange_kernel, n_local, norm), out_sha...]
where the time goes in v9:
time: 28 us; the launch traced here: 27.9 us
  Pallas kernels  25.2 us (90%)
  local copies, waits for them, and re-layouts  2.04 us (7%)
  between operations  0.65 us (2%)
    pallas_call x1, Pallas kernels, exchanged(): pl.pallas_call(functools.partial(exchange_kernel, n_local, norm), out_sha...  25.2 us
    unnamed x4, local copies, waits for them, and re-layouts  2.04 us

profile of v9, /device:TPU:0, one launch (start us, length us, event | category | flops | bytes accessed | tf_op | source)
XLA Modules:
  0.0 27.9 jit_solution(8318146565561936414)
XLA Ops:
  0.6 25.2 %shard_map.59 = (bf16[128,128]{1,0:T(8,128)(2,1)}, f32[128,128]{1,0:T(8,128)}) custom-call(bf16[128,4096]{1,0:T(8,128)(2,1)} %act_hbm.1, bf16[4,256,128]{2,1,0:T(8,128)(2,1)} %codes_hbm.1, f32[4,128]{1,0:T(4,128)} %scales_hbm.1, bf16[128,128]{1,0:T(8,128)(2,1)} %cot_hbm.1), custom_call_target="tpu_custom_call" | custom-call | flops 268435456 | bytes 1048576 | tf_op jit(solution)/shard_map/pallas_call | solution.py:244
  25.8 0.0 copy-start
  25.8 1.4 %copy.8 = bf16[128,128]{1,0:T(8,128)(2,1)} copy(bf16[128,128]{1,0:T(8,128)(2,1)} %get-tuple-element.4) | data formatting | bytes 65536
  27.3 0.0 copy-done
  27.3 0.6 %copy.9 = f32[128,128]{1,0:T(8,128)} copy(f32[128,128]{1,0:T(8,128)S(1)} %copy-done) | data formatting | bytes 131072
Async XLA Ops:
  25.8 1.4 %copy-start = (f32[128,128]{1,0:T(8,128)S(1)}, f32[128,128]{1,0:T(8,128)}, u32[]{:S(2)}) copy-start(f32[128,128]{1,0:T(8,128)} %get-tuple-element.5) | copy-start | bytes 196612

commit v10 on v9

--- a/solution.py
+++ b/solution.py
@@ -128,9 +128,30 @@
     def half_of(of_core):
         return pl.ds(aligned(of_core, half), half)
 
-    def line_copy(k, to):
-        part = half_of(core)
-        return send(weight.at[part], weight_in.at[k, part], w_send.at[k], w_recv.at[k], node, to)
+    def line_copy(src, slot, send_sem, to):
+        return send(src, weight_in.at[slot, half_of(core)], send_sem, w_recv.at[slot], node, to)
+
+    def line_own(rightward):
+        src = weight.at[half_of(core)]
+        if rightward:
+            return line_copy(src, 0, w_send.at[0], (z + 1) % n_local)
+        return line_copy(src, last - 1, w_send.at[1], (z + last) % n_local)
+
+    def line_on(k, rightward):
+        src = weight_in.at[k, half_of(core)]
+        if rightward:
+            return line_copy(src, k + 1, w_send.at[2 + k], (z + 1) % n_local)
+        return line_copy(src, k - 1, w_send.at[2 + k], (z + last) % n_local)
+
+    def on_line(act_on):
+        pl.when(z < last)(lambda: act_on(line_own(True)))
+        pl.when(z > 0)(lambda: act_on(line_own(False)))
+
+    def on_relay(k, act_on):
+        if k + 1 < last:
+            pl.when((k < z) & (z < last))(lambda: act_on(line_on(k, True)))
+        if k > 0:
+            pl.when((k >= z) & (z > 0))(lambda: act_on(line_on(k, False)))
 
     def pass_copy(k, of_core):
         ref = weight_in.at[k, half_of(of_core)]
@@ -147,8 +168,7 @@
     for b in range(blocks):
         part = codes_ref[b].astype(F32) * scales_ref[b : b + 1, :]
         weight[b * block : (b + 1) * block, :] = part.astype(BF16)
-    for k, to, _ in line:
-        line_copy(k, to).start()
+    on_line(lambda copy: copy.start())
     loads[3].wait()
     for i in range(8):
         for j in range(n_local):
@@ -199,22 +219,28 @@
         total[...] += jnp.dot(act[:, pl.ds(column, half)], weight_in[k, half_of(of_core)],
                               preferred_element_type=F32)
 
-    group_term(0)
-    for k in range(1, last):
+    def relay(distance):
+        for k, _, owner in line:
+            if min(k, last - 1 - k) == distance:
+                line_copy(weight.at[half_of(core)], k, w_send.at[0], (z + 1) % n_local).wait_recv()
+                on_relay(k, lambda copy: copy.start())
+                pass_copy(k, core).start()
+                add_half(k, owner, core)
+
+    for k in range(last):
         group_term(k)
-        finish_term(k - 1)
-    for k, to, owner in line:
-        line_copy(k, to).wait_recv()
-        pass_copy(k, core).start()
-        add_half(k, owner, core)
+        relay(k)
+        if k > 0:
+            finish_term(k - 1)
     finish_term(last - 1)
     group_term(last)
     for copy in cot_copies + cot_passes:
         copy.wait_send()
     for k in range(n_local):
         act_whole(k).wait_send()
+    on_line(lambda copy: copy.wait_send())
     for k, to, owner in line:
-        line_copy(k, to).wait_send()
+        on_relay(k, lambda copy: copy.wait_send())
         pass_copy(k, 1 - core).wait_recv()
         add_half(k, owner, 1 - core)
     values_ref[...] = total[...].astype(BF16)
@@ -263,7 +289,7 @@
             piece, piece, piece, piece,
             pltpu.VMEM((tok, head), F32),
             dma((4,)), dma((n_local,)), dma((n_local,)), dma((5,)), dma((5,)),
-            dma((n_local,)), dma((n_local,)), dma((n_local,)), dma((n_local,)),
+            dma((n_local + 1,)), dma((n_local,)), dma((n_local,)), dma((n_local,)),
             dma((n_local,)), dma((n_local,)),
             dma((n_local,)), dma((n_local,)),
         ],

time: 28 us -> 34.8 us (1.24)
  Pallas kernels: 25.2 us -> 32 us
    pallas_call x1, Pallas kernels: 25.2 us -> 32 us  [exchanged(): pl.pallas_call(functools.partial(exchange_kernel, n_local, norm), out_sha...]
where the time goes in v10:
time: 34.8 us; the launch traced here: 34.7 us
  Pallas kernels  32 us (92%)
  local copies, waits for them, and re-layouts  2.04 us (6%)
  between operations  0.65 us (2%)
    pallas_call x1, Pallas kernels, exchanged(): pl.pallas_call(functools.partial(exchange_kernel, n_local, norm), out_sha...  32 us
    unnamed x4, local copies, waits for them, and re-layouts  2.04 us

profile of v10, /device:TPU:0, one launch (start us, length us, event | category | flops | bytes accessed | tf_op | source)
XLA Modules:
  0.0 34.7 jit_solution(4996005336945913116)
XLA Ops:
  0.6 32.0 %shard_map.59 = (bf16[128,128]{1,0:T(8,128)(2,1)}, f32[128,128]{1,0:T(8,128)}) custom-call(bf16[128,4096]{1,0:T(8,128)(2,1)} %act_hbm.1, bf16[4,256,128]{2,1,0:T(8,128)(2,1)} %codes_hbm.1, f32[4,128]{1,0:T(4,128)} %scales_hbm.1, bf16[128,128]{1,0:T(8,128)(2,1)} %cot_hbm.1), custom_call_target="tpu_custom_call" | custom-call | flops 268435456 | bytes 1048576 | tf_op jit(solution)/shard_map/pallas_call | solution.py:270
  32.6 0.0 copy-start
  32.6 1.4 %copy.8 = bf16[128,128]{1,0:T(8,128)(2,1)} copy(bf16[128,128]{1,0:T(8,128)(2,1)} %get-tuple-element.4) | data formatting | bytes 65536
  34.0 0.0 copy-done
  34.0 0.6 %copy.9 = f32[128,128]{1,0:T(8,128)} copy(f32[128,128]{1,0:T(8,128)S(1)} %copy-done) | data formatting | bytes 131072
Async XLA Ops:
  32.6 1.4 %copy-start = (f32[128,128]{1,0:T(8,128)S(1)}, f32[128,128]{1,0:T(8,128)}, u32[]{:S(2)}) copy-start(f32[128,128]{1,0:T(8,128)} %get-tuple-element.5) | copy-start | bytes 196612

commit v11 on v9

--- a/solution.py
+++ b/solution.py
@@ -171,8 +171,8 @@
                 copy.wait_recv()
                 if i < 2:
                     cot_passes[i].start()
-            if n_local > 2:
-                for copy in act_copies(2):
+            for later in range(2, n_local):
+                for copy in act_copies(later):
                     copy.start()
         act_whole(k).wait_recv()
         if k == 0:
@@ -183,9 +183,6 @@
         cot = jnp.concatenate([cot_in[begin + i] for i in range(4)], axis=1)
         other_out[k] = jnp.dot(cot, act_in[k, 1 - mine], preferred_element_type=F32)
         sum_copy(k).start()
-        if k + 3 < n_local:
-            for copy in act_copies(k + 3):
-                copy.start()
         term_out[k] = jnp.dot(cot, act_in[k, mine], preferred_element_type=F32)
 
     def finish_term(k):
@@ -203,10 +200,11 @@
     for k in range(1, last):
         group_term(k)
         finish_term(k - 1)
-    for k, to, owner in line:
-        line_copy(k, to).wait_recv()
-        pass_copy(k, core).start()
-        add_half(k, owner, core)
+        if k == 1:
+            for i, to, owner in line:
+                line_copy(i, to).wait_recv()
+                pass_copy(i, core).start()
+                add_half(i, owner, core)
     finish_term(last - 1)
     group_term(last)
     for copy in cot_copies + cot_passes:
@@ -298,7 +296,7 @@
         share = activations.shape[1] // (n_node * n_local)
         rows = codes.shape[0] * codes.shape[1]
         tok = activations.shape[0]
-        fits = n_node == 8 and n_local > 1 and share % 128 == 0 and rows % 256 == 0 and tok % 128 == 0
+        fits = n_node == 8 and n_local > 2 and share % 128 == 0 and rows % 256 == 0 and tok % 128 == 0
         run = exchanged if fits else gathered
         return run(n_node, n_local, activations, codes, scales, cotangent)
 

time: 28 us -> 29.8 us (1.064)
  Pallas kernels: 25.2 us -> 26.9 us
    pallas_call x1, Pallas kernels: 25.2 us -> 26.9 us  [exchanged(): pl.pallas_call(functools.partial(exchange_kernel, n_local, norm), out_sha...]
where the time goes in v11:
time: 29.8 us; the launch traced here: 29.6 us
  Pallas kernels  26.9 us (90%)
  local copies, waits for them, and re-layouts  2.04 us (7%)
  between operations  0.65 us (2%)
    pallas_call x1, Pallas kernels, exchanged(): pl.pallas_call(functools.partial(exchange_kernel, n_local, norm), out_sha...  26.9 us
    unnamed x4, local copies, waits for them, and re-layouts  2.04 us

profile of v11, /device:TPU:0, one launch (start us, length us, event | category | flops | bytes accessed | tf_op | source)
XLA Modules:
  0.0 29.6 jit_solution(9845194877707039022)
XLA Ops:
  0.6 26.9 %shard_map.59 = (bf16[128,128]{1,0:T(8,128)(2,1)}, f32[128,128]{1,0:T(8,128)}) custom-call(bf16[128,4096]{1,0:T(8,128)(2,1)} %act_hbm.1, bf16[4,256,128]{2,1,0:T(8,128)(2,1)} %codes_hbm.1, f32[4,128]{1,0:T(4,128)} %scales_hbm.1, bf16[128,128]{1,0:T(8,128)(2,1)} %cot_hbm.1), custom_call_target="tpu_custom_call" | custom-call | flops 268435456 | bytes 1048576 | tf_op jit(solution)/shard_map/pallas_call | solution.py:242
  27.6 0.0 copy-start
  27.6 1.4 %copy.8 = bf16[128,128]{1,0:T(8,128)(2,1)} copy(bf16[128,128]{1,0:T(8,128)(2,1)} %get-tuple-element.4) | data formatting | bytes 65536
  29.0 0.0 copy-done
  29.0 0.6 %copy.9 = f32[128,128]{1,0:T(8,128)} copy(f32[128,128]{1,0:T(8,128)S(1)} %copy-done) | data formatting | bytes 131072
Async XLA Ops:
  27.6 1.4 %copy-start = (f32[128,128]{1,0:T(8,128)S(1)}, f32[128,128]{1,0:T(8,128)}, u32[]{:S(2)}) copy-start(f32[128,128]{1,0:T(8,128)} %get-tuple-element.5) | copy-start | bytes 196612

commit v12 on v9

--- a/solution.py
+++ b/solution.py
@@ -203,12 +203,12 @@
     for k in range(1, last):
         group_term(k)
         finish_term(k - 1)
+    finish_term(last - 1)
+    group_term(last)
     for k, to, owner in line:
         line_copy(k, to).wait_recv()
         pass_copy(k, core).start()
         add_half(k, owner, core)
-    finish_term(last - 1)
-    group_term(last)
     for copy in cot_copies + cot_passes:
         copy.wait_send()
     for k in range(n_local):

time: 28 us -> 27.7 us (0.989)
  Pallas kernels: 25.2 us -> 24.9 us
    pallas_call x1, Pallas kernels: 25.2 us -> 24.9 us  [exchanged(): pl.pallas_call(functools.partial(exchange_kernel, n_local, norm), out_sha...]
where the time goes in v12:
time: 27.7 us; the launch traced here: 27.6 us
  Pallas kernels  24.9 us (90%)
  local copies, waits for them, and re-layouts  2.04 us (7%)
  between operations  0.65 us (2%)
    pallas_call x1, Pallas kernels, exchanged(): pl.pallas_call(functools.partial(exchange_kernel, n_local, norm), out_sha...  24.9 us
    unnamed x4, local copies, waits for them, and re-layouts  2.04 us

profile of v12, /device:TPU:0, one launch (start us, length us, event | category | flops | bytes accessed | tf_op | source)
XLA Modules:
  0.0 27.6 jit_solution(14451413262012922723)
XLA Ops:
  0.6 24.9 %shard_map.59 = (bf16[128,128]{1,0:T(8,128)(2,1)}, f32[128,128]{1,0:T(8,128)}) custom-call(bf16[128,4096]{1,0:T(8,128)(2,1)} %act_hbm.1, bf16[4,256,128]{2,1,0:T(8,128)(2,1)} %codes_hbm.1, f32[4,128]{1,0:T(4,128)} %scales_hbm.1, bf16[128,128]{1,0:T(8,128)(2,1)} %cot_hbm.1), custom_call_target="tpu_custom_call" | custom-call | flops 268435456 | bytes 1048576 | tf_op jit(solution)/shard_map/pallas_call | solution.py:244
  25.5 0.0 copy-start
  25.5 1.4 %copy.8 = bf16[128,128]{1,0:T(8,128)(2,1)} copy(bf16[128,128]{1,0:T(8,128)(2,1)} %get-tuple-element.4) | data formatting | bytes 65536
  26.9 0.0 copy-done
  26.9 0.6 %copy.9 = f32[128,128]{1,0:T(8,128)} copy(f32[128,128]{1,0:T(8,128)S(1)} %copy-done) | data formatting | bytes 131072
Async XLA Ops:
  25.5 1.4 %copy-start = (f32[128,128]{1,0:T(8,128)S(1)}, f32[128,128]{1,0:T(8,128)}, u32[]{:S(2)}) copy-start(f32[128,128]{1,0:T(8,128)} %get-tuple-element.5) | copy-start | bytes 196612

commit v13 on v12

--- a/solution.py
+++ b/solution.py
@@ -171,9 +171,6 @@
                 copy.wait_recv()
                 if i < 2:
                     cot_passes[i].start()
-            if n_local > 2:
-                for copy in act_copies(2):
-                    copy.start()
         act_whole(k).wait_recv()
         if k == 0:
             for copy in cot_passes:
@@ -183,8 +180,8 @@
         cot = jnp.concatenate([cot_in[begin + i] for i in range(4)], axis=1)
         other_out[k] = jnp.dot(cot, act_in[k, 1 - mine], preferred_element_type=F32)
         sum_copy(k).start()
-        if k + 3 < n_local:
-            for copy in act_copies(k + 3):
+        if k + 2 < n_local:
+            for copy in act_copies(k + 2):
                 copy.start()
         term_out[k] = jnp.dot(cot, act_in[k, mine], preferred_element_type=F32)
 

time: 27.7 us -> 28.3 us (1.022)
  Pallas kernels: 24.9 us -> 25.4 us
    pallas_call x1, Pallas kernels: 24.9 us -> 25.4 us  [exchanged(): pl.pallas_call(functools.partial(exchange_kernel, n_local, norm), out_sha...]
where the time goes in v13:
time: 28.3 us; the launch traced here: 28.1 us
  Pallas kernels  25.4 us (90%)
  local copies, waits for them, and re-layouts  2.04 us (7%)
  between operations  0.65 us (2%)
    pallas_call x1, Pallas kernels, exchanged(): pl.pallas_call(functools.partial(exchange_kernel, n_local, norm), out_sha...  25.4 us
    unnamed x4, local copies, waits for them, and re-layouts  2.04 us

profile of v13, /device:TPU:0, one launch (start us, length us, event | category | flops | bytes accessed | tf_op | source)
XLA Modules:
  0.0 28.1 jit_solution(15160127957980025225)
XLA Ops:
  0.6 25.4 %shard_map.59 = (bf16[128,128]{1,0:T(8,128)(2,1)}, f32[128,128]{1,0:T(8,128)}) custom-call(bf16[128,4096]{1,0:T(8,128)(2,1)} %act_hbm.1, bf16[4,256,128]{2,1,0:T(8,128)(2,1)} %codes_hbm.1, f32[4,128]{1,0:T(4,128)} %scales_hbm.1, bf16[128,128]{1,0:T(8,128)(2,1)} %cot_hbm.1), custom_call_target="tpu_custom_call" | custom-call | flops 268435456 | bytes 1048576 | tf_op jit(solution)/shard_map/pallas_call | solution.py:241
  26.1 0.0 copy-start
  26.1 1.4 %copy.8 = bf16[128,128]{1,0:T(8,128)(2,1)} copy(bf16[128,128]{1,0:T(8,128)(2,1)} %get-tuple-element.4) | data formatting | bytes 65536
  27.5 0.0 copy-done
  27.5 0.6 %copy.9 = f32[128,128]{1,0:T(8,128)} copy(f32[128,128]{1,0:T(8,128)S(1)} %copy-done) | data formatting | bytes 131072
Async XLA Ops:
  26.1 1.4 %copy-start = (f32[128,128]{1,0:T(8,128)S(1)}, f32[128,128]{1,0:T(8,128)}, u32[]{:S(2)}) copy-start(f32[128,128]{1,0:T(8,128)} %get-tuple-element.5) | copy-start | bytes 196612
